TPU v7x, 32 devices: a whole 2x2x4 slice. The times are simulated.
32 devices in a mesh: seq: 16 (over z, y, core), head: 2 (over x).
Axes of the slice: x: 2, y: 2, z: 4, core: 2. Of those that a mesh axis runs over, the one named last changes fastest.
Arguments:
- queries: bfloat16 [4096, 4096], P('seq', 'head'), may hold values from -0.29882812 to 0.29882812
- keys: bfloat16 [4096, 4096], P('seq', 'head'), may hold values from -0.29882812 to 0.29882812
- values: bfloat16 [4096, 4096], P('seq', 'head'), may hold values from -0.59765625 to 0.59765625
- out_grad: bfloat16 [4096, 4096], P('seq', 'head'), may hold values from -6 to 6
- doc_lengths: int32 [8], replicated, may hold values from 1 to 1024, 4096 in all
Outputs:
- query_grad: bfloat16 [4096, 4096], P(('seq', 'head'))
- key_grad: bfloat16 [4096, 4096], P(('seq', 'head'))
- value_grad: bfloat16 [4096, 4096], P(('seq', 'head'))
Inputs may be any that keep to these rules, and one draw needn't show every extreme that they name: `doc_lengths`: the lengths sum to 4096 and the largest equals 1024.
All inputs are finite; a program needn't handle non-finite values.
Results may differ from a plain program's by a relative error of at most 0.0033.
Values may be sent and summed in bfloat16 or wider, within the bound.
No kernel may reach another device: no remote copies, remote signals or barrier semaphores. Data moves between devices by JAX's collectives and lax.ppermute only.
A program may use at most 128 MiB of HBM per device.

v0:
```python
import functools

import jax
import jax.numpy as jnp
from jax import lax
from jax.experimental import pallas as pl
from jax.experimental.pallas import tpu as pltpu
from jax.sharding import PartitionSpec as P

HEAD_DIM = 128
MOST = 1024
GROUP = 4
CHUNK = 4
LINK = jnp.bfloat16
VMEM_LIMIT = 16 * 1024 * 1024
GRAD_LIMIT = 48 * 1024 * 1024
FIRST_LIMIT = 52 * 1024 * 1024
NT = (((1,), (1,)), ((), ()))
TN = (((0,), (0,)), ((), ()))
NN = (((1,), (0,)), ((), ()))


def dot(a, b, dims):
    return lax.dot_general(a, b, dims, preferred_element_type=jnp.float32)


def doc_at(meta, ndocs, position):
    start, begin, end = jnp.int32(0), jnp.int32(0), jnp.int32(0)
    for i in range(ndocs):
        stop = start + meta[i]
        begin = jnp.where(start <= position, start, begin)
        end = jnp.where(start <= position, stop, end)
        start = stop
    return begin, end


def block_range(meta, ndocs, base, rows):
    begin0, end0 = doc_at(meta, ndocs, base)
    begin1, end1 = doc_at(meta, ndocs, base + rows - 1)
    first = jnp.where(begin0 < base, end0, base) - base
    return begin0, end0, begin1, end1, first, begin1 - base


def state_kernel(lengths, q, k, v, g, *rest, ndocs, rows, offset, heads, group):
    kept, sent, held, sems = rest[-4:]
    gw = group * HEAD_DIM
    copies = []
    for c in range(heads // group):
        for i, ref in enumerate((q, k, v, g)):
            src = ref.at[:, pl.ds(offset + c * gw, gw)]
            copies.append(pltpu.make_async_copy(src, held.at[i, :, pl.ds(c * gw, gw)], sems.at[c, i]))
            copies[-1].start()
    place = lax.axis_index("seq")
    first_core = lax.rem(place, 2) == 0
    _, _, _, _, first, last = block_range(lengths, ndocs, place * rows, rows)
    order = lax.broadcasted_iota(jnp.int32, (rows, HEAD_DIM), 0)
    first_rows, last_rows = order < first, order >= last
    zero = jnp.zeros((), held.dtype)

    def one(h):
        cols = slice(h * HEAD_DIM, (h + 1) * HEAD_DIM)
        tail = dot(jnp.where(last_rows, held[1, :, cols], zero), held[2, :, cols], TN)
        return tail, dot(jnp.where(first_rows, held[0, :, cols], zero), held[3, :, cols], TN)

    for h in range(heads):
        if h % group == 0:
            for copy in copies[4 * h // group:4 * h // group + 4]:
                copy.wait()
        tail, head = one(h)
        kept[h] = jnp.where(first_core, tail, head)
        sent[h] = jnp.where(first_core, head, tail)


def pair_kernel(lengths, kept, got, *rest, ndocs, rows):
    sent = rest[-1]
    place = lax.axis_index("seq")
    first_core = lax.rem(place, 2) == 0
    even = (place - lax.rem(place, 2)) * rows
    odd = even + rows
    _, even_e0 = doc_at(lengths, ndocs, even)
    odd_b1, _ = doc_at(lengths, ndocs, odd + rows - 1)
    joins = jnp.where(jnp.where(first_core, odd_b1 < odd, even_e0 > odd), 1.0, 0.0)
    sent[...] = (got[...] + joins * kept[...]).astype(LINK)


def join_kernel(lengths, other, *rest, ndocs, rows, counts, hops):
    came, mine, theirs = rest[:hops], rest[-2 * len(counts):-len(counts)], rest[-len(counts):]
    place = lax.axis_index("seq")
    first_core = lax.rem(place, 2) == 0
    even = (place - lax.rem(place, 2)) * rows
    odd = even + rows
    even_b0, _ = doc_at(lengths, ndocs, even)
    _, even_e1 = doc_at(lengths, ndocs, odd - 1)
    odd_b0, _ = doc_at(lengths, ndocs, odd)
    _, odd_e1 = doc_at(lengths, ndocs, odd + rows - 1)

    def one(if_first, if_second):
        return jnp.where(jnp.where(first_core, if_first, if_second), 1.0, 0.0)

    weights = [
        one(odd + rows + hop * 2 * rows < odd_e1, even - hop * 2 * rows > even_b0) for hop in range(hops)
    ]
    from_other, from_pair = one(odd < even_e1, odd > odd_b0), one(odd + rows < even_e1, even > odd_b0)
    for c, count in enumerate(counts):
        at = slice(sum(counts[:c]), sum(counts[:c + 1]))
        total = weights[0] * came[0][at].astype(jnp.float32)
        for hop in range(1, hops):
            total = total + weights[hop] * came[hop][at].astype(jnp.float32)
        theirs[c][...] = total
        mine[c][...] = from_other * other[at] + from_pair * total


def split(a, axis):
    high = a.astype(jnp.bfloat16)
    return jnp.concatenate([high, (a - high.astype(jnp.float32)).astype(jnp.bfloat16)], axis=axis)


def grad_kernel(lengths, q, k, v, g, mine, got, *rest, ndocs, rows, heads, groups):
    outs, lower, upper, done = rest[-3 - groups:-3], rest[-3], rest[-2], rest[-1]
    place, column = lax.axis_index("seq"), lax.axis_index("head")
    base = place * rows

    @pl.when(pl.program_id(0) == 0)
    def _():
        line = lax.broadcasted_iota(jnp.int32, (rows, rows), 0)
        across = lax.broadcasted_iota(jnp.int32, (rows, rows), 1)
        begin_line = jnp.zeros((rows, rows), jnp.int32)
        begin_across = jnp.zeros((rows, rows), jnp.int32)
        start = jnp.int32(0) - base
        for i in range(ndocs):
            begin_line = jnp.where(line >= start, start, begin_line)
            begin_across = jnp.where(across >= start, start, begin_across)
            start = start + lengths[i]
        lower[...] = jnp.where((across <= line) & (across >= begin_line), 1, 0)
        upper[...] = jnp.where((line <= across) & (line >= begin_across), 1, 0)

    first_core = lax.rem(place, 2) == 0
    _, _, _, _, first, last = block_range(lengths, ndocs, base, rows)
    order = lax.broadcasted_iota(jnp.int32, (rows, HEAD_DIM), 0)
    first_rows, last_rows = order < first, order >= last
    in_lower, in_upper = lower[...] == 1, upper[...] == 1
    for h in range(heads):
        cols = slice(h * HEAD_DIM, (h + 1) * HEAD_DIM)
        state = jnp.where(first_core, got[h], mine[h])
        grad = jnp.where(first_core, mine[h], got[h])
        qh, kh, vh, gh = (ref[:, cols] for ref in (q, k, v, g))
        k2, v2, g2 = (jnp.concatenate([a, a], axis=1) for a in (kh, vh, gh))
        weight_gv = jnp.where(in_lower, dot(gh, vh, NT), 0.0).astype(jnp.bfloat16)
        weight_vg = jnp.where(in_upper, dot(vh, gh, NT), 0.0).astype(jnp.bfloat16)
        weight_kq = jnp.where(in_upper, dot(kh, qh, NT), 0.0).astype(jnp.bfloat16)
        carry_q = jnp.where(first_rows, dot(g2, split(state, 1), NT), 0.0)
        carry_k = jnp.where(last_rows, dot(v2, split(grad, 1), NT), 0.0)
        carry_v = jnp.where(last_rows, dot(k2, split(grad, 0), NN), 0.0)
        done[0, :, cols] = (dot(weight_gv, kh, NN) + carry_q).astype(jnp.bfloat16)
        done[1, :, cols] = (dot(weight_vg, qh, NN) + carry_k).astype(jnp.bfloat16)
        done[2, :, cols] = (dot(weight_kq, gh, NN) + carry_v).astype(jnp.bfloat16)
    part = rows // groups
    for j in range(groups):
        at = pl.ds(pl.multiple_of(lax.rem(column + j, groups) * part, part), part)
        for i in range(3):
            outs[j][i] = done[i, at, :]


def place_kernel(*refs, groups, offset, cw, width):
    parts, outs, sems = refs[:groups], refs[-4:-1], refs[-1]
    column = lax.axis_index("head")
    copies = []
    for j in range(groups):
        start = pl.multiple_of(lax.rem(column + groups - j, groups) * width + offset, 128)
        for i in range(3):
            copies.append(pltpu.make_async_copy(parts[j].at[i], outs[i].at[:, pl.ds(start, cw)], sems.at[len(copies)]))
            copies[-1].start()
    for copy in copies:
        copy.wait()


def cuts_of(width):
    heads = width // HEAD_DIM
    size = CHUNK if heads % (2 * CHUNK) == 0 else 2
    cw, half = size * HEAD_DIM, max(heads // 2, size) * HEAD_DIM
    return [(at, half, [(o, cw) for o in range(at, at + half, cw)]) for at in range(0, width, half)]


def shards(queries, keys, values, out_grad, doc_lengths):
    rows, width = queries.shape
    ndocs = doc_lengths.shape[0]
    seq, groups = lax.axis_size("seq"), lax.axis_size("head")
    pairs = seq // 2
    hops = -(-MOST // (2 * rows))
    halves = cuts_of(width)
    step = 2 * HEAD_DIM
    part = rows // groups
    anywhere = pl.BlockSpec(memory_space=pl.ANY)
    in_vmem = pl.BlockSpec(memory_space=pltpu.VMEM)
    in_smem = pl.BlockSpec(memory_space=pltpu.SMEM)
    f32, bf16 = jnp.float32, jnp.bfloat16
    inputs = (queries, keys, values, out_grad)
    sizes = dict(ndocs=ndocs, rows=rows)
    cheap = pl.CostEstimate(flops=0, bytes_accessed=1024, transcendentals=0)

    def shape_of(*dims, dtype=f32):
        return jax.ShapeDtypeStruct(dims, dtype)

    def call(name, kernel, args, outs, scratch=(), after=()):
        return pl.pallas_call(
            kernel, in_specs=[in_smem] + [in_vmem] * len(args) + [anywhere] * len(after), out_specs=[in_vmem] * len(outs), out_shape=outs,
            scratch_shapes=list(scratch), cost_estimate=cheap,
            compiler_params=pltpu.CompilerParams(vmem_limit_bytes=VMEM_LIMIT), name=name,
        )(doc_lengths, *args, *after)

    def swap_cores(a):
        return lax.ppermute(a, "seq", [(b, b ^ 1) for b in range(seq)])

    def swap_pairs(sent):
        came = []
        for hop in range(1, hops + 1):
            perm = [(2 * m, 2 * (m + hop) + 1) for m in range(pairs - hop)]
            came.append(lax.ppermute(sent, "seq", perm + [(b, a) for a, b in perm]))
        return came

    def send_rows(outs):
        arrived = list(outs[:1])
        for j in range(1, groups):
            arrived.append(lax.ppermute(outs[j], "head", [(x, (x + j) % groups) for x in range(groups)]))
        return arrived

    square = (HEAD_DIM, HEAD_DIM)

    def states(offset, half, after):
        heads = half // HEAD_DIM
        group = GROUP if heads % GROUP == 0 else 2
        kept, sent = pl.pallas_call(
            functools.partial(state_kernel, offset=offset, heads=heads, group=group, **sizes),
            in_specs=[in_smem] + [anywhere] * (4 + len(after)), out_specs=[in_vmem] * 2,
            out_shape=[shape_of(heads, *square)] * 2,
            scratch_shapes=[pltpu.VMEM((4, rows, half), bf16), pltpu.SemaphoreType.DMA((heads // group, 4))],
            cost_estimate=cheap, compiler_params=pltpu.CompilerParams(vmem_limit_bytes=FIRST_LIMIT), name="states",
        )(doc_lengths, *inputs, *after)
        return kept, swap_cores(sent)

    def pair_up(kept, got, after):
        out = shape_of(*kept.shape, dtype=LINK)
        return swap_pairs(call("pair", functools.partial(pair_kernel, **sizes), (kept, got), [out], after=after)[0])

    def join(kept, came, chunks, after):
        counts = [cw // HEAD_DIM for _, cw in chunks]
        joined = call(
            "join", functools.partial(join_kernel, counts=counts, hops=hops, **sizes), (swap_cores(kept), *came),
            [shape_of(n, *square) for n in counts] * 2, after=after,
        )
        return [(mine, swap_cores(theirs)) for mine, theirs in zip(joined[:len(chunks)], joined[len(chunks):])]

    def grads(offset, cw, mine, theirs, after):
        block = pl.BlockSpec((rows, step), lambda s, lengths: (0, offset // step + s))
        state_block = pl.BlockSpec((2,) + square, lambda s, lengths: (s, 0, 0))
        out_block = pl.BlockSpec((3, part, step), lambda s, lengths: (0, 0, s))
        return pl.pallas_call(
            functools.partial(grad_kernel, heads=2, groups=groups, **sizes),
            grid_spec=pltpu.PrefetchScalarGridSpec(
                num_scalar_prefetch=1, grid=(cw // step,),
                in_specs=[block] * 4 + [state_block] * 2 + [anywhere] * len(after), out_specs=[out_block] * groups,
                scratch_shapes=[pltpu.VMEM((rows, rows), jnp.int32)] * 2 + [pltpu.VMEM((3, rows, step), bf16)],
            ),
            out_shape=[shape_of(3, part, cw, dtype=bf16)] * groups, cost_estimate=cheap,
            compiler_params=pltpu.CompilerParams(vmem_limit_bytes=GRAD_LIMIT), name="grads",
        )(doc_lengths, *inputs, mine, theirs, *after)

    own = []
    for offset, half, _ in halves:
        own.append(states(offset, half, [kept for kept, _ in own[-1:]]))
    cuts, sent, arrived = [], [], []
    for (kept, got), (_, _, chunks) in zip(own, halves):
        came = pair_up(kept, got, [outs[0] for outs in sent[:1]])
        for (offset, cw), (mine, theirs) in zip(chunks, join(kept, came, chunks, [parts[1] for parts in arrived[:1]])):
            sent.append(grads(offset, cw, mine, theirs, [outs[0] for outs in sent[-1:]] + [parts[1] for parts in arrived[1:-1]][-1:]))
            arrived.append(send_rows(sent[-1]))
        cuts += chunks

    placed = []
    for c, (offset, cw) in enumerate(cuts):
        placed = pl.pallas_call(
            functools.partial(place_kernel, groups=groups, offset=offset, cw=cw, width=width),
            grid_spec=pl.GridSpec(
                grid=(1,), in_specs=[anywhere] * (groups + len(placed)), out_specs=[anywhere] * 3,
                scratch_shapes=[pltpu.SemaphoreType.DMA((3 * groups,))],
            ),
            out_shape=[shape_of(part, width * groups, dtype=bf16)] * 3,
            input_output_aliases={groups + i: i for i in range(len(placed))},
            cost_estimate=cheap,
            compiler_params=pltpu.CompilerParams(vmem_limit_bytes=VMEM_LIMIT), name="place",
        )(*arrived[c], *placed)
    return tuple(placed)


def solution(mesh):
    return jax.shard_map(
        shards,
        mesh=mesh,
        in_specs=(P("seq", "head"), P("seq", "head"), P("seq", "head"), P("seq", "head"), P()),
        out_specs=(P(("seq", "head"), None), P(("seq", "head"), None), P(("seq", "head"), None)),
        check_vma=False,
    )
```

profile of v0, /device:TPU:0, one launch (start us, length us, event | category | flops | bytes accessed | tf_op | source)
XLA Modules:
  0.0 63.9 jit_solution(4795377979108886139)
XLA Ops:
  0.6 0.0 copy-start.4
  0.6 0.6 %copy-done.4 = s32[8]{0:T(128)S(1)} copy-done((s32[8]{0:T(128)S(1)}, s32[8]{0:T(128)}, u32[]{:S(2)}) %copy-start.4) | copy-done | bytes 56
  1.3 2.6 %states.2 = (f32[8,128,128]{2,1,0:T(8,128)S(1)}, f32[8,128,128]{2,1,0:T(8,128)S(1)}) custom-call(s32[8]{0:T(128)S(1)} %copy-done.4, bf16[256,2048]{1,0:T(8,128)(2,1)} %q.11, bf16[256,2048]{1,0:T(8,128)(2,1)} %k.11, bf16[256,2048]{1,0:T(8,128)(2,1)} %v.11, bf16[256,2048]{1,0:T(8,128)(2,1)} %g.11), custom_call_target="tpu_custom_call" | custom-call | bytes 1024 | tf_op jit(solution)/shard_map/states/pallas_call | solution.py:232
  3.9 0.5 collective-permute-start.3
  4.4 0.1 collective-permute-start.2
  4.5 1.5 %collective-permute-done.3.got = f32[8,128,128]{2,1,0:T(8,128)S(1)} collective-permute-done((f32[8,128,128]{2,1,0:T(8,128)S(1)}, f32[8,128,128]{2,1,0:T(8,128)S(1)}, u32[]{:S(2)}, u32[]{:S(2)}) %collective-permute-start.3) | collective-permute-done | bytes 524320 | tf_op jit(solution)/shard_map/ppermute | solution.py:212
  5.9 0.6 pair.2
  6.5 4.5 %collective-permute-start.4 = (bf16[8,128,128]{2,1,0:T(8,128)(2,1)S(1)}, bf16[8,128,128]{2,1,0:T(8,128)(2,1)S(1)}, u32[]{:S(2)}, u32[]{:S(2)}) collective-permute-start(bf16[8,128,128]{2,1,0:T(8,128)(2,1)S(1)} %pair.2), channel_id=1, source_target_pairs={{0,6},{4,10},{8,14},{12,18},{16,22},{20,26},{24,30},{6,0},{10,4},{... | collective-permute-start | bytes 786440 | tf_op jit(solution)/shard_map/ppermute | solution.py:218
  11.1 3.3 %collective-permute-start.5 = (bf16[8,128,128]{2,1,0:T(8,128)(2,1)S(1)}, bf16[8,128,128]{2,1,0:T(8,128)(2,1)S(1)}, u32[]{:S(2)}, u32[]{:S(2)}) collective-permute-start(bf16[8,128,128]{2,1,0:T(8,128)(2,1)S(1)} %pair.2), channel_id=1, source_target_pairs={{0,10},{4,14},{8,18},{12,22},{16,26},{20,30},{10,0},{14,4},{18,8},... | collective-permute-start | bytes 786440 | tf_op jit(solution)/shard_map/ppermute | solution.py:218
  14.4 0.0 copy-start.1
  14.4 0.0 copy-start.2
  14.5 0.0 copy-start.3
  14.5 2.8 %states.3 = (f32[8,128,128]{2,1,0:T(8,128)S(1)}, f32[8,128,128]{2,1,0:T(8,128)S(1)}) custom-call(s32[8]{0:T(128)S(1)} %copy-done.4, bf16[256,2048]{1,0:T(8,128)(2,1)} %q.11, bf16[256,2048]{1,0:T(8,128)(2,1)} %k.11, bf16[256,2048]{1,0:T(8,128)(2,1)} %v.11, bf16[256,2048]{1,0:T(8,128)(2,1)} %g.11, f32[8,128,128]{2,1,0:T(8,128)S(1)} %get-tuple-element.32.rest_0_.kept), custom_call_target="tpu_custom_call" | custom-call | bytes 1024 | tf_op jit(solution)/shard_map/states/pallas_call | solution.py:232
  17.3 0.0 copy-start
  17.3 0.1 collective-permute-start.1
  17.4 0.0 collective-permute-done.2.other
  17.4 0.3 collective-permute-done.4.rest_0_
  17.8 1.6 %collective-permute-done.5.rest_1_ = bf16[8,128,128]{2,1,0:T(8,128)(2,1)S(1)} collective-permute-done((bf16[8,128,128]{2,1,0:T(8,128)(2,1)S(1)}, bf16[8,128,128]{2,1,0:T(8,128)(2,1)S(1)}, u32[]{:S(2)}, u32[]{:S(2)}) %collective-permute-start.5) | collective-permute-done | bytes 262176 | tf_op jit(solution)/shard_map/ppermute | solution.py:218
  19.4 0.7 %join.2 = (f32[4,128,128]{2,1,0:T(8,128)S(1)}, f32[4,128,128]{2,1,0:T(8,128)S(1)}, f32[4,128,128]{2,1,0:T(8,128)S(1)}, f32[4,128,128]{2,1,0:T(8,128)S(1)}) custom-call(s32[8]{0:T(128)S(1)} %copy-done.4, f32[8,128,128]{2,1,0:T(8,128)S(1)} %collective-permute-done.2.other, bf16[8,128,128]{2,1,0:T(8,128)(2,1)S(1)} %collective-permute-done.4.rest_0_, ...), custom_call_target="tpu_custom_call" | custom-call | bytes 1024 | tf_op jit(solution)/shard_map/join/pallas_call | solution.py:205
  20.1 0.1 collective-permute-start.6
  20.2 0.5 collective-permute-start
  20.7 1.0 %collective-permute-done.6.got = f32[4,128,128]{2,1,0:T(8,128)S(1)} collective-permute-done((f32[4,128,128]{2,1,0:T(8,128)S(1)}, f32[4,128,128]{2,1,0:T(8,128)S(1)}, u32[]{:S(2)}, u32[]{:S(2)}) %collective-permute-start.6) | collective-permute-done | bytes 262176 | tf_op jit(solution)/shard_map/ppermute | solution.py:212
  21.7 0.0 copy-done.1
  21.7 0.0 copy-done.2
  21.7 0.0 copy-done.3
  21.7 0.0 copy-done
  21.7 2.7 %grads.4 = (bf16[3,128,512]{2,1,0:T(8,128)(2,1)S(1)}, bf16[3,128,512]{2,1,0:T(8,128)(2,1)S(1)}) custom-call(s32[8]{0:T(128)S(1)} %copy-done.4, bf16[256,2048]{1,0:T(8,128)(2,1)S(1)} %copy-done, bf16[256,2048]{1,0:T(8,128)(2,1)S(1)} %copy-done.1, bf16[256,2048]{1,0:T(8,128)(2,1)S(1)} %copy-done.2, bf16[256,2048]{1,0:T(8,128)(2,1)S(1)} %copy-done.3, ...), custom_call_target="tpu_custom_call" | custom-call | bytes 1024 | tf_op jit(solution)/shard_map/grads/pallas_call | solution.py:257
  24.5 1.6 %collective-permute-start.9 = (bf16[3,128,512]{2,1,0:T(8,128)(2,1)S(1)}, bf16[3,128,512]{2,1,0:T(8,128)(2,1)S(1)}, u32[]{:S(2)}, u32[]{:S(2)}) collective-permute-start(bf16[3,128,512]{2,1,0:T(8,128)(2,1)S(1)} %get-tuple-element.39), channel_id=1, source_target_pairs={{0,1},{1,0},{2,3},{3,2},{4,5},{5,4},{6,7},{7,6},{8,9},{9,8},{10,11... | collective-permute-start | bytes 1179656 | tf_op jit(solution)/shard_map/ppermute | solution.py:224
  26.1 0.0 collective-permute-start.12
  26.1 0.0 collective-permute-done.1.got
  26.1 0.6 pair.3
  26.7 2.9 %collective-permute-start.7 = (bf16[8,128,128]{2,1,0:T(8,128)(2,1)S(1)}, bf16[8,128,128]{2,1,0:T(8,128)(2,1)S(1)}, u32[]{:S(2)}, u32[]{:S(2)}) collective-permute-start(bf16[8,128,128]{2,1,0:T(8,128)(2,1)S(1)} %pair.3), channel_id=1, source_target_pairs={{0,6},{4,10},{8,14},{12,18},{16,22},{20,26},{24,30},{6,0},{10,4},{... | collective-permute-start | bytes 786440 | tf_op jit(solution)/shard_map/ppermute | solution.py:218
  29.6 3.0 %collective-permute-start.8 = (bf16[8,128,128]{2,1,0:T(8,128)(2,1)S(1)}, bf16[8,128,128]{2,1,0:T(8,128)(2,1)S(1)}, u32[]{:S(2)}, u32[]{:S(2)}) collective-permute-start(bf16[8,128,128]{2,1,0:T(8,128)(2,1)S(1)} %pair.3), channel_id=1, source_target_pairs={{0,10},{4,14},{8,18},{12,22},{16,26},{20,30},{10,0},{14,4},{18,8},... | collective-permute-start | bytes 786440 | tf_op jit(solution)/shard_map/ppermute | solution.py:218
  32.6 0.0 collective-permute-done.12.got
  32.6 2.8 %grads.5 = (bf16[3,128,512]{2,1,0:T(8,128)(2,1)S(1)}, bf16[3,128,512]{2,1,0:T(8,128)(2,1)S(1)}) custom-call(s32[8]{0:T(128)S(1)} %copy-done.4, bf16[256,2048]{1,0:T(8,128)(2,1)S(1)} %copy-done, bf16[256,2048]{1,0:T(8,128)(2,1)S(1)} %copy-done.1, bf16[256,2048]{1,0:T(8,128)(2,1)S(1)} %copy-done.2, bf16[256,2048]{1,0:T(8,128)(2,1)S(1)} %copy-done.3, ...), custom_call_target="tpu_custom_call" | custom-call | bytes 1024 | tf_op jit(solution)/shard_map/grads/pallas_call | solution.py:257
  35.4 0.6 collective-permute-start.13
  36.0 0.0 collective-permute-done.other
  36.0 0.3 collective-permute-done.7.rest_0_
  36.3 1.3 %collective-permute-done.8.rest_1_ = bf16[8,128,128]{2,1,0:T(8,128)(2,1)S(1)} collective-permute-done((bf16[8,128,128]{2,1,0:T(8,128)(2,1)S(1)}, bf16[8,128,128]{2,1,0:T(8,128)(2,1)S(1)}, u32[]{:S(2)}, u32[]{:S(2)}) %collective-permute-start.8) | collective-permute-done | bytes 262176 | tf_op jit(solution)/shard_map/ppermute | solution.py:218
  37.6 0.0 collective-permute-done.9.rest_2_.refs_1_
  37.6 0.7 %join.3 = (f32[4,128,128]{2,1,0:T(8,128)S(1)}, f32[4,128,128]{2,1,0:T(8,128)S(1)}, f32[4,128,128]{2,1,0:T(8,128)S(1)}, f32[4,128,128]{2,1,0:T(8,128)S(1)}) custom-call(s32[8]{0:T(128)S(1)} %copy-done.4, f32[8,128,128]{2,1,0:T(8,128)S(1)} %collective-permute-done.other, bf16[8,128,128]{2,1,0:T(8,128)(2,1)S(1)} %collective-permute-done.7.rest_0_, ...), custom_call_target="tpu_custom_call" | custom-call | bytes 1024 | tf_op jit(solution)/shard_map/join/pallas_call | solution.py:205
  38.3 0.1 collective-permute-start.11
  38.4 0.5 collective-permute-start.10
  38.9 1.0 %collective-permute-done.11.got = f32[4,128,128]{2,1,0:T(8,128)S(1)} collective-permute-done((f32[4,128,128]{2,1,0:T(8,128)S(1)}, f32[4,128,128]{2,1,0:T(8,128)S(1)}, u32[]{:S(2)}, u32[]{:S(2)}) %collective-permute-start.11) | collective-permute-done | bytes 262176 | tf_op jit(solution)/shard_map/ppermute | solution.py:212
  39.9 0.0 copy-start.5
  39.9 0.7 %copy-done.5 = s32[8]{0:T(128)S(1)} copy-done((s32[8]{0:T(128)S(1)}, s32[8]{0:T(128)}, u32[]{:S(2)}) %copy-start.5) | copy-done | bytes 56
  40.5 2.8 %grads.6 = (bf16[3,128,512]{2,1,0:T(8,128)(2,1)S(1)}, bf16[3,128,512]{2,1,0:T(8,128)(2,1)S(1)}) custom-call(s32[8]{0:T(128)S(1)} %copy-done.5, bf16[256,2048]{1,0:T(8,128)(2,1)S(1)} %copy-done, bf16[256,2048]{1,0:T(8,128)(2,1)S(1)} %copy-done.1, bf16[256,2048]{1,0:T(8,128)(2,1)S(1)} %copy-done.2, bf16[256,2048]{1,0:T(8,128)(2,1)S(1)} %copy-done.3, ...), custom_call_target="tpu_custom_call" | custom-call | bytes 1024 | tf_op jit(solution)/shard_map/grads/pallas_call | solution.py:257
  43.3 0.6 collective-permute-start.15
  43.9 0.2 collective-permute-done.13.rest_1_.refs_1_
  44.1 0.0 collective-permute-done.10.got
  44.1 3.5 %grads.7 = (bf16[3,128,512]{2,1,0:T(8,128)(2,1)S(1)}, bf16[3,128,512]{2,1,0:T(8,128)(2,1)S(1)}) custom-call(s32[8]{0:T(128)S(1)} %copy-done.5, bf16[256,2048]{1,0:T(8,128)(2,1)S(1)} %copy-done, bf16[256,2048]{1,0:T(8,128)(2,1)S(1)} %copy-done.1, bf16[256,2048]{1,0:T(8,128)(2,1)S(1)} %copy-done.2, bf16[256,2048]{1,0:T(8,128)(2,1)} %g.11, ...), custom_call_target="tpu_custom_call" | custom-call | bytes 1024 | tf_op jit(solution)/shard_map/grads/pallas_call | solution.py:257
  47.7 1.6 %collective-permute-start.14 = (bf16[3,128,512]{2,1,0:T(8,128)(2,1)S(1)}, bf16[3,128,512]{2,1,0:T(8,128)(2,1)S(1)}, u32[]{:S(2)}, u32[]{:S(2)}) collective-permute-start(bf16[3,128,512]{2,1,0:T(8,128)(2,1)S(1)} %get-tuple-element.50), channel_id=1, source_target_pairs={{0,1},{1,0},{2,3},{3,2},{4,5},{5,4},{6,7},{7,6},{8,9},{9,8},{10,11... | collective-permute-start | bytes 1179656 | tf_op jit(solution)/shard_map/ppermute | solution.py:224
  49.3 0.9 %place.4 = (bf16[128,4096]{1,0:T(8,128)(2,1)}, bf16[128,4096]{1,0:T(8,128)(2,1)}, bf16[128,4096]{1,0:T(8,128)(2,1)}) custom-call(bf16[3,128,512]{2,1,0:T(8,128)(2,1)S(1)} %get-tuple-element.38.rest_0_.refs_0_, bf16[3,128,512]{2,1,0:T(8,128)(2,1)S(1)} %collective-permute-done.9.rest_2_.refs_1_), custom_call_target="tpu_custom_call" | custom-call | bytes 1024 | tf_op jit(solution)/shard_map/place/pallas_call | solution.py:281
  50.2 0.9 %place.5 = (bf16[128,4096]{1,0:T(8,128)(2,1)}, bf16[128,4096]{1,0:T(8,128)(2,1)}, bf16[128,4096]{1,0:T(8,128)(2,1)}) custom-call(bf16[3,128,512]{2,1,0:T(8,128)(2,1)S(1)} %get-tuple-element.46.rest_0_.refs_0_, bf16[3,128,512]{2,1,0:T(8,128)(2,1)S(1)} %collective-permute-done.13.rest_1_.refs_1_, ...), custom_call_target="tpu_custom_call", output_to_operand_aliasing={{0}: (2, {}), {1}: (3, {}), {2}: (4, {})} | custom-call | bytes 1024 | tf_op jit(solution)/shard_map/place/pallas_call | solution.py:281
  51.1 4.2 %collective-permute-done.15.refs_1_ = bf16[3,128,512]{2,1,0:T(8,128)(2,1)S(1)} collective-permute-done((bf16[3,128,512]{2,1,0:T(8,128)(2,1)S(1)}, bf16[3,128,512]{2,1,0:T(8,128)(2,1)S(1)}, u32[]{:S(2)}, u32[]{:S(2)}) %collective-permute-start.15) | collective-permute-done | bytes 393248 | tf_op jit(solution)/shard_map/ppermute | solution.py:224
  55.3 0.9 %place.6 = (bf16[128,4096]{1,0:T(8,128)(2,1)}, bf16[128,4096]{1,0:T(8,128)(2,1)}, bf16[128,4096]{1,0:T(8,128)(2,1)}) custom-call(bf16[3,128,512]{2,1,0:T(8,128)(2,1)S(1)} %get-tuple-element.47.rest_0_.refs_0_, bf16[3,128,512]{2,1,0:T(8,128)(2,1)S(1)} %collective-permute-done.15.refs_1_, ...), custom_call_target="tpu_custom_call", output_to_operand_aliasing={{0}: (2, {}), {1}: (3, {}), {2}: (4, {})} | custom-call | bytes 1024 | tf_op jit(solution)/shard_map/place/pallas_call | solution.py:281
  56.3 6.7 %collective-permute-done.14.refs_1_ = bf16[3,128,512]{2,1,0:T(8,128)(2,1)S(1)} collective-permute-done((bf16[3,128,512]{2,1,0:T(8,128)(2,1)S(1)}, bf16[3,128,512]{2,1,0:T(8,128)(2,1)S(1)}, u32[]{:S(2)}, u32[]{:S(2)}) %collective-permute-start.14) | collective-permute-done | bytes 393248 | tf_op jit(solution)/shard_map/ppermute | solution.py:224
  63.0 0.9 %place.7 = (bf16[128,4096]{1,0:T(8,128)(2,1)}, bf16[128,4096]{1,0:T(8,128)(2,1)}, bf16[128,4096]{1,0:T(8,128)(2,1)}) custom-call(bf16[3,128,512]{2,1,0:T(8,128)(2,1)S(1)} %get-tuple-element.49.refs_0_, bf16[3,128,512]{2,1,0:T(8,128)(2,1)S(1)} %collective-permute-done.14.refs_1_, ...), custom_call_target="tpu_custom_call", output_to_operand_aliasing={{0}: (2, {}), {1}: (3, {}), {2}: (4, {})} | custom-call | bytes 1024 | tf_op jit(solution)/shard_map/place/pallas_call | solution.py:281
Async XLA Ops:
  0.6 0.7 %copy-start.4 = (s32[8]{0:T(128)S(1)}, s32[8]{0:T(128)}, u32[]{:S(2)}) copy-start(s32[8]{0:T(128)} %lengths.19) | copy-start | bytes 100
  3.9 2.1 %collective-permute-start.3 = (f32[8,128,128]{2,1,0:T(8,128)S(1)}, f32[8,128,128]{2,1,0:T(8,128)S(1)}, u32[]{:S(2)}, u32[]{:S(2)}) collective-permute-start(f32[8,128,128]{2,1,0:T(8,128)S(1)} %get-tuple-element.35), channel_id=1, source_target_pairs={{0,2},{2,0},{4,6},{6,4},{8,10},{10,8},{12,14},{14,12},{16,18},{18,... | collective-permute-start | bytes 1572872 | tf_op jit(solution)/shard_map/ppermute | solution.py:212
  4.4 13.0 %collective-permute-start.2 = (f32[8,128,128]{2,1,0:T(8,128)S(1)}, f32[8,128,128]{2,1,0:T(8,128)S(1)}, u32[]{:S(2)}, u32[]{:S(2)}) collective-permute-start(f32[8,128,128]{2,1,0:T(8,128)S(1)} %get-tuple-element.32.rest_0_.kept), channel_id=1, source_target_pairs={{0,2},{2,0},{4,6},{6,4},{8,10},{10,8},{12,14},{14,12},{16,18},{18,... | collective-permute-start | bytes 1572872 | tf_op jit(solution)/shard_map/ppermute | solution.py:212
  6.5 11.2 %collective-permute-start.4 = (bf16[8,128,128]{2,1,0:T(8,128)(2,1)S(1)}, bf16[8,128,128]{2,1,0:T(8,128)(2,1)S(1)}, u32[]{:S(2)}, u32[]{:S(2)}) collective-permute-start(bf16[8,128,128]{2,1,0:T(8,128)(2,1)S(1)} %pair.2), channel_id=1, source_target_pairs={{0,6},{4,10},{8,14},{12,18},{16,22},{20,26},{24,30},{6,0},{10,4},{... | collective-permute-start | bytes 786440 | tf_op jit(solution)/shard_map/ppermute | solution.py:218
  11.1 8.3 %collective-permute-start.5 = (bf16[8,128,128]{2,1,0:T(8,128)(2,1)S(1)}, bf16[8,128,128]{2,1,0:T(8,128)(2,1)S(1)}, u32[]{:S(2)}, u32[]{:S(2)}) collective-permute-start(bf16[8,128,128]{2,1,0:T(8,128)(2,1)S(1)} %pair.2), channel_id=1, source_target_pairs={{0,10},{4,14},{8,18},{12,22},{16,26},{20,30},{10,0},{14,4},{18,8},... | collective-permute-start | bytes 786440 | tf_op jit(solution)/shard_map/ppermute | solution.py:218
  14.4 7.3 %copy-start.1 = (bf16[256,2048]{1,0:T(8,128)(2,1)S(1)}, bf16[256,2048]{1,0:T(8,128)(2,1)}, u32[]{:S(2)}) copy-start(bf16[256,2048]{1,0:T(8,128)(2,1)} %k.11) | copy-start | bytes 3145732
  14.4 7.3 %copy-start.2 = (bf16[256,2048]{1,0:T(8,128)(2,1)S(1)}, bf16[256,2048]{1,0:T(8,128)(2,1)}, u32[]{:S(2)}) copy-start(bf16[256,2048]{1,0:T(8,128)(2,1)} %v.11) | copy-start | bytes 3145732
  14.5 7.3 %copy-start.3 = (bf16[256,2048]{1,0:T(8,128)(2,1)S(1)}, bf16[256,2048]{1,0:T(8,128)(2,1)}, u32[]{:S(2)}) copy-start(bf16[256,2048]{1,0:T(8,128)(2,1)} %g.11) | copy-start | bytes 3145732
  17.3 4.4 %copy-start = (bf16[256,2048]{1,0:T(8,128)(2,1)S(1)}, bf16[256,2048]{1,0:T(8,128)(2,1)}, u32[]{:S(2)}) copy-start(bf16[256,2048]{1,0:T(8,128)(2,1)} %q.11) | copy-start | bytes 3145732
  17.3 8.7 %collective-permute-start.1 = (f32[8,128,128]{2,1,0:T(8,128)S(1)}, f32[8,128,128]{2,1,0:T(8,128)S(1)}, u32[]{:S(2)}, u32[]{:S(2)}) collective-permute-start(f32[8,128,128]{2,1,0:T(8,128)S(1)} %get-tuple-element.34), channel_id=1, source_target_pairs={{0,2},{2,0},{4,6},{6,4},{8,10},{10,8},{12,14},{14,12},{16,18},{18,... | collective-permute-start | bytes 1572872 | tf_op jit(solution)/shard_map/ppermute | solution.py:212
  20.1 1.6 %collective-permute-start.6 = (f32[4,128,128]{2,1,0:T(8,128)S(1)}, f32[4,128,128]{2,1,0:T(8,128)S(1)}, u32[]{:S(2)}, u32[]{:S(2)}) collective-permute-start(f32[4,128,128]{2,1,0:T(8,128)S(1)} %get-tuple-element.37), channel_id=1, source_target_pairs={{0,2},{2,0},{4,6},{6,4},{8,10},{10,8},{12,14},{14,12},{16,18},{18,... | collective-permute-start | bytes 786440 | tf_op jit(solution)/shard_map/ppermute | solution.py:212
  20.2 15.8 %collective-permute-start = (f32[8,128,128]{2,1,0:T(8,128)S(1)}, f32[8,128,128]{2,1,0:T(8,128)S(1)}, u32[]{:S(2)}, u32[]{:S(2)}) collective-permute-start(f32[8,128,128]{2,1,0:T(8,128)S(1)} %get-tuple-element.33.kept), channel_id=1, source_target_pairs={{0,2},{2,0},{4,6},{6,4},{8,10},{10,8},{12,14},{14,12},{16,18},{18,... | collective-permute-start | bytes 1572872 | tf_op jit(solution)/shard_map/ppermute | solution.py:212
  24.5 13.1 %collective-permute-start.9 = (bf16[3,128,512]{2,1,0:T(8,128)(2,1)S(1)}, bf16[3,128,512]{2,1,0:T(8,128)(2,1)S(1)}, u32[]{:S(2)}, u32[]{:S(2)}) collective-permute-start(bf16[3,128,512]{2,1,0:T(8,128)(2,1)S(1)} %get-tuple-element.39), channel_id=1, source_target_pairs={{0,1},{1,0},{2,3},{3,2},{4,5},{5,4},{6,7},{7,6},{8,9},{9,8},{10,11... | collective-permute-start | bytes 1179656 | tf_op jit(solution)/shard_map/ppermute | solution.py:224
  26.1 6.5 %collective-permute-start.12 = (f32[4,128,128]{2,1,0:T(8,128)S(1)}, f32[4,128,128]{2,1,0:T(8,128)S(1)}, u32[]{:S(2)}, u32[]{:S(2)}) collective-permute-start(f32[4,128,128]{2,1,0:T(8,128)S(1)} %get-tuple-element.45), channel_id=1, source_target_pairs={{0,2},{2,0},{4,6},{6,4},{8,10},{10,8},{12,14},{14,12},{16,18},{18,... | collective-permute-start | bytes 786440 | tf_op jit(solution)/shard_map/ppermute | solution.py:212
  26.7 9.6 %collective-permute-start.7 = (bf16[8,128,128]{2,1,0:T(8,128)(2,1)S(1)}, bf16[8,128,128]{2,1,0:T(8,128)(2,1)S(1)}, u32[]{:S(2)}, u32[]{:S(2)}) collective-permute-start(bf16[8,128,128]{2,1,0:T(8,128)(2,1)S(1)} %pair.3), channel_id=1, source_target_pairs={{0,6},{4,10},{8,14},{12,18},{16,22},{20,26},{24,30},{6,0},{10,4},{... | collective-permute-start | bytes 786440 | tf_op jit(solution)/shard_map/ppermute | solution.py:218
  29.6 8.0 %collective-permute-start.8 = (bf16[8,128,128]{2,1,0:T(8,128)(2,1)S(1)}, bf16[8,128,128]{2,1,0:T(8,128)(2,1)S(1)}, u32[]{:S(2)}, u32[]{:S(2)}) collective-permute-start(bf16[8,128,128]{2,1,0:T(8,128)(2,1)S(1)} %pair.3), channel_id=1, source_target_pairs={{0,10},{4,14},{8,18},{12,22},{16,26},{20,30},{10,0},{14,4},{18,8},... | collective-permute-start | bytes 786440 | tf_op jit(solution)/shard_map/ppermute | solution.py:218
  35.4 8.8 %collective-permute-start.13 = (bf16[3,128,512]{2,1,0:T(8,128)(2,1)S(1)}, bf16[3,128,512]{2,1,0:T(8,128)(2,1)S(1)}, u32[]{:S(2)}, u32[]{:S(2)}) collective-permute-start(bf16[3,128,512]{2,1,0:T(8,128)(2,1)S(1)} %get-tuple-element.48), channel_id=1, source_target_pairs={{0,1},{1,0},{2,3},{3,2},{4,5},{5,4},{6,7},{7,6},{8,9},{9,8},{10,11... | collective-permute-start | bytes 1179656 | tf_op jit(solution)/shard_map/ppermute | solution.py:224
  38.3 1.6 %collective-permute-start.11 = (f32[4,128,128]{2,1,0:T(8,128)S(1)}, f32[4,128,128]{2,1,0:T(8,128)S(1)}, u32[]{:S(2)}, u32[]{:S(2)}) collective-permute-start(f32[4,128,128]{2,1,0:T(8,128)S(1)} %get-tuple-element.43), channel_id=1, source_target_pairs={{0,2},{2,0},{4,6},{6,4},{8,10},{10,8},{12,14},{14,12},{16,18},{18,... | collective-permute-start | bytes 786440 | tf_op jit(solution)/shard_map/ppermute | solution.py:212
  38.4 5.8 %collective-permute-start.10 = (f32[4,128,128]{2,1,0:T(8,128)S(1)}, f32[4,128,128]{2,1,0:T(8,128)S(1)}, u32[]{:S(2)}, u32[]{:S(2)}) collective-permute-start(f32[4,128,128]{2,1,0:T(8,128)S(1)} %get-tuple-element.41), channel_id=1, source_target_pairs={{0,2},{2,0},{4,6},{6,4},{8,10},{10,8},{12,14},{14,12},{16,18},{18,... | collective-permute-start | bytes 786440 | tf_op jit(solution)/shard_map/ppermute | solution.py:212
  39.9 0.7 %copy-start.5 = (s32[8]{0:T(128)S(1)}, s32[8]{0:T(128)}, u32[]{:S(2)}) copy-start(s32[8]{0:T(128)} %lengths.19) | copy-start | bytes 100
  43.3 12.0 %collective-permute-start.15 = (bf16[3,128,512]{2,1,0:T(8,128)(2,1)S(1)}, bf16[3,128,512]{2,1,0:T(8,128)(2,1)S(1)}, u32[]{:S(2)}, u32[]{:S(2)}) collective-permute-start(bf16[3,128,512]{2,1,0:T(8,128)(2,1)S(1)} %get-tuple-element.51), channel_id=1, source_target_pairs={{0,1},{1,0},{2,3},{3,2},{4,5},{5,4},{6,7},{7,6},{8,9},{9,8},{10,11... | collective-permute-start | bytes 1179656 | tf_op jit(solution)/shard_map/ppermute | solution.py:224
  47.7 15.3 %collective-permute-start.14 = (bf16[3,128,512]{2,1,0:T(8,128)(2,1)S(1)}, bf16[3,128,512]{2,1,0:T(8,128)(2,1)S(1)}, u32[]{:S(2)}, u32[]{:S(2)}) collective-permute-start(bf16[3,128,512]{2,1,0:T(8,128)(2,1)S(1)} %get-tuple-element.50), channel_id=1, source_target_pairs={{0,1},{1,0},{2,3},{3,2},{4,5},{5,4},{6,7},{7,6},{8,9},{9,8},{10,11... | collective-permute-start | bytes 1179656 | tf_op jit(solution)/shard_map/ppermute | solution.py:224
where the time goes:
time: 64.2 us; the launch traced here: 63.9 us
  Pallas kernels  23.6 us (37%)
  starting transfers between devices  19.9 us (31%)
  waiting for transfers between devices  18.2 us (28%)
  local copies, waits for them, and re-layouts  1.33 us (2%)
  between operations  0.86 us (1%)
    ppermute x4, starting transfers between devices, swap_pairs(): came.append(lax.ppermute(sent, 'seq', perm + [(b, a) for a, b in perm]))  13.8 us
    pallas_call x4, Pallas kernels, grads(): pl.pallas_call(functools.partial(grad_kernel, heads=2, groups=groups, **s...  11.8 us
    ppermute x4, waiting for transfers between devices, send_rows(): lax.ppermute(outs[j], 'head', [(x, (x + j) % groups) for x in range(group...  11.1 us
    pallas_call x2, Pallas kernels, states(): pl.pallas_call(functools.partial(state_kernel, offset=offset, heads=heads...  5.4 us
    ppermute x4, starting transfers between devices, send_rows(): lax.ppermute(outs[j], 'head', [(x, (x + j) % groups) for x in range(group...  4.32 us
    pallas_call x4, Pallas kernels, shards(): pl.pallas_call(functools.partial(place_kernel, groups=groups, offset=offs...  3.7 us
    ppermute x4, waiting for transfers between devices, swap_pairs(): came.append(lax.ppermute(sent, 'seq', perm + [(b, a) for a, b in perm]))  3.56 us
    ppermute x8, waiting for transfers between devices, swap_cores(): return lax.ppermute(a, 'seq', [(b, b ^ 1) for b in range(seq)])  3.52 us
  transfers between devices with their start and end apart: 16, of which 10 were waited for; matrix products, arithmetic and copies ran while one was open for 0% of the time, Pallas kernels for 31%

commit v1 on v0

--- a/solution.py
+++ b/solution.py
@@ -14,6 +14,7 @@
 LINK = jnp.bfloat16
 VMEM_LIMIT = 16 * 1024 * 1024
 GRAD_LIMIT = 48 * 1024 * 1024
+LOCAL_LIMIT = 52 * 1024 * 1024
 FIRST_LIMIT = 52 * 1024 * 1024
 NT = (((1,), (1,)), ((), ()))
 TN = (((0,), (0,)), ((), ()))
@@ -115,6 +116,65 @@
     return jnp.concatenate([high, (a - high.astype(jnp.float32)).astype(jnp.bfloat16)], axis=axis)
 
 
+def masks(lengths, lower, upper, ndocs, rows):
+    line = lax.broadcasted_iota(jnp.int32, (rows, rows), 0)
+    across = lax.broadcasted_iota(jnp.int32, (rows, rows), 1)
+    begin_line = jnp.zeros((rows, rows), jnp.int32)
+    begin_across = jnp.zeros((rows, rows), jnp.int32)
+    start = jnp.int32(0) - lax.axis_index("seq") * rows
+    for i in range(ndocs):
+        begin_line = jnp.where(line >= start, start, begin_line)
+        begin_across = jnp.where(across >= start, start, begin_across)
+        start = start + lengths[i]
+    lower[...] = jnp.where((across <= line) & (across >= begin_line), 1, 0)
+    upper[...] = jnp.where((line <= across) & (line >= begin_across), 1, 0)
+
+
+def local_kernel(lengths, q, k, v, g, *rest, ndocs, rows, heads):
+    near, kvg, token, lower, upper = rest[-5:]
+    token[...] = jnp.zeros_like(token)
+    for i, ref in enumerate((k, v, g)):
+        kvg[i] = ref[...]
+
+    @pl.when(pl.program_id(0) == 0)
+    def _():
+        masks(lengths, lower, upper, ndocs, rows)
+
+    for h in range(heads):
+        cols = slice(h * HEAD_DIM, (h + 1) * HEAD_DIM)
+        qh, kh, vh, gh = (ref[:, cols] for ref in (q, k, v, g))
+        weight_gv = jnp.where(lower[...] == 1, dot(gh, vh, NT), 0.0).astype(jnp.bfloat16)
+        weight_vg = jnp.where(upper[...] == 1, dot(vh, gh, NT), 0.0).astype(jnp.bfloat16)
+        weight_kq = jnp.where(upper[...] == 1, dot(kh, qh, NT), 0.0).astype(jnp.bfloat16)
+        near[0, :, cols] = dot(weight_gv, kh, NN)
+        near[1, :, cols] = dot(weight_vg, qh, NN)
+        near[2, :, cols] = dot(weight_kq, gh, NN)
+
+
+def carry_kernel(lengths, near, kvg, mine, got, *rest, ndocs, rows, heads, groups):
+    outs, done = rest[-1 - groups:-1], rest[-1]
+    place, column = lax.axis_index("seq"), lax.axis_index("head")
+    first_core = lax.rem(place, 2) == 0
+    _, _, _, _, first, last = block_range(lengths, ndocs, place * rows, rows)
+    order = lax.broadcasted_iota(jnp.int32, (rows, HEAD_DIM), 0)
+    first_rows, last_rows = order < first, order >= last
+    for h in range(heads):
+        cols = slice(h * HEAD_DIM, (h + 1) * HEAD_DIM)
+        state = jnp.where(first_core, got[h], mine[h])
+        grad = jnp.where(first_core, mine[h], got[h])
+        k2, v2, g2 = (jnp.concatenate([kvg[i, :, cols]] * 2, axis=1) for i in range(3))
+        carry_q = jnp.where(first_rows, dot(g2, split(state, 1), NT), 0.0)
+        carry_k = jnp.where(last_rows, dot(v2, split(grad, 1), NT), 0.0)
+        carry_v = jnp.where(last_rows, dot(k2, split(grad, 0), NN), 0.0)
+        for i, carry in enumerate((carry_q, carry_k, carry_v)):
+            done[i, :, cols] = (near[i, :, cols] + carry).astype(jnp.bfloat16)
+    part = rows // groups
+    for j in range(groups):
+        at = pl.ds(pl.multiple_of(lax.rem(column + j, groups) * part, part), part)
+        for i in range(3):
+            outs[j][i] = done[i, at, :]
+
+
 def grad_kernel(lengths, q, k, v, g, mine, got, *rest, ndocs, rows, heads, groups):
     outs, lower, upper, done = rest[-3 - groups:-3], rest[-3], rest[-2], rest[-1]
     place, column = lax.axis_index("seq"), lax.axis_index("head")
@@ -122,17 +182,7 @@
 
     @pl.when(pl.program_id(0) == 0)
     def _():
-        line = lax.broadcasted_iota(jnp.int32, (rows, rows), 0)
-        across = lax.broadcasted_iota(jnp.int32, (rows, rows), 1)
-        begin_line = jnp.zeros((rows, rows), jnp.int32)
-        begin_across = jnp.zeros((rows, rows), jnp.int32)
-        start = jnp.int32(0) - base
-        for i in range(ndocs):
-            begin_line = jnp.where(line >= start, start, begin_line)
-            begin_across = jnp.where(across >= start, start, begin_across)
-            start = start + lengths[i]
-        lower[...] = jnp.where((across <= line) & (across >= begin_line), 1, 0)
-        upper[...] = jnp.where((line <= across) & (line >= begin_across), 1, 0)
+        masks(lengths, lower, upper, ndocs, rows)
 
     first_core = lax.rem(place, 2) == 0
     _, _, _, _, first, last = block_range(lengths, ndocs, base, rows)
@@ -229,18 +279,18 @@
     def states(offset, half, after):
         heads = half // HEAD_DIM
         group = GROUP if heads % GROUP == 0 else 2
-        kept, sent = pl.pallas_call(
+        return pl.pallas_call(
             functools.partial(state_kernel, offset=offset, heads=heads, group=group, **sizes),
             in_specs=[in_smem] + [anywhere] * (4 + len(after)), out_specs=[in_vmem] * 2,
             out_shape=[shape_of(heads, *square)] * 2,
             scratch_shapes=[pltpu.VMEM((4, rows, half), bf16), pltpu.SemaphoreType.DMA((heads // group, 4))],
             cost_estimate=cheap, compiler_params=pltpu.CompilerParams(vmem_limit_bytes=FIRST_LIMIT), name="states",
         )(doc_lengths, *inputs, *after)
-        return kept, swap_cores(sent)
 
     def pair_up(kept, got, after):
         out = shape_of(*kept.shape, dtype=LINK)
-        return swap_pairs(call("pair", functools.partial(pair_kernel, **sizes), (kept, got), [out], after=after)[0])
+        total = call("pair", functools.partial(pair_kernel, **sizes), (kept, got), [out], after=after)[0]
+        return total, swap_pairs(total)
 
     def join(kept, came, chunks, after):
         counts = [cw // HEAD_DIM for _, cw in chunks]
@@ -265,15 +315,45 @@
             compiler_params=pltpu.CompilerParams(vmem_limit_bytes=GRAD_LIMIT), name="grads",
         )(doc_lengths, *inputs, mine, theirs, *after)
 
-    own = []
-    for offset, half, _ in halves:
-        own.append(states(offset, half, [kept for kept, _ in own[-1:]]))
-    cuts, sent, arrived = [], [], []
-    for (kept, got), (_, _, chunks) in zip(own, halves):
-        came = pair_up(kept, got, [outs[0] for outs in sent[:1]])
-        for (offset, cw), (mine, theirs) in zip(chunks, join(kept, came, chunks, [parts[1] for parts in arrived[:1]])):
-            sent.append(grads(offset, cw, mine, theirs, [outs[0] for outs in sent[-1:]] + [parts[1] for parts in arrived[1:-1]][-1:]))
-            arrived.append(send_rows(sent[-1]))
+    def local(offset, cw, after):
+        block = pl.BlockSpec((rows, step), lambda s, lengths: (0, offset // step + s))
+        out_block = pl.BlockSpec((3, rows, step), lambda s, lengths: (0, 0, s))
+        return pl.pallas_call(
+            functools.partial(local_kernel, heads=2, **sizes),
+            grid_spec=pltpu.PrefetchScalarGridSpec(
+                num_scalar_prefetch=1, grid=(cw // step,), in_specs=[block] * 4 + [anywhere] * len(after),
+                out_specs=[out_block] * 2 + [pl.BlockSpec((8, 128), lambda s, lengths: (0, 0))],
+                scratch_shapes=[pltpu.VMEM((rows, rows), jnp.int32)] * 2,
+            ),
+            out_shape=[shape_of(3, rows, cw), shape_of(3, rows, cw, dtype=bf16), shape_of(8, 128)], cost_estimate=cheap,
+            compiler_params=pltpu.CompilerParams(vmem_limit_bytes=LOCAL_LIMIT), name="local",
+        )(doc_lengths, *inputs, *after)
+
+    def carry(near, kvg, mine, theirs, cw, after):
+        kernel = functools.partial(carry_kernel, heads=cw // HEAD_DIM, groups=groups, **sizes)
+        return call(
+            "carry", kernel, (near, kvg, mine, theirs), [shape_of(3, part, cw, dtype=bf16)] * groups,
+            [pltpu.VMEM((3, rows, cw), bf16)], after,
+        )
+
+    cuts, near, outs, arrived, total = [], [], [], [], None
+    for start, half, chunks in halves:
+        early = total is None
+        kept, sent = states(start, half, [] if early else [total])
+        if early:
+            near.append(local(*chunks[0], [kept]))
+        total, came = pair_up(kept, swap_cores(sent), near[0][2:] if early else [outs[0][0]])
+        if early:
+            for chunk in chunks[1:]:
+                near.append(local(*chunk, [total]))
+        joined = join(kept, came, chunks, [made[2] for made in near[1:]] if early else [arrived[0][1]])
+        for c, ((offset, cw), (mine, theirs)) in enumerate(zip(chunks, joined)):
+            after = [made[0] for made in outs[-1:]] + [parts[1] for parts in arrived[1:-1]][-1:]
+            if early:
+                outs.append(carry(*near[c][:2], mine, theirs, cw, after))
+            else:
+                outs.append(grads(offset, cw, mine, theirs, after))
+            arrived.append(send_rows(outs[-1]))
         cuts += chunks
 
     placed = []

time: 64.2 us -> 66.6 us (1.037)
  Pallas kernels: 23.6 us -> 28.5 us
  waiting for transfers between devices: 18.2 us -> 16.2 us
    pallas_call x0 -> x2, Pallas kernels: none -> 8.16 us  [local(): pl.pallas_call(functools.partial(local_kernel, heads=2, **sizes), grid_sp...]
    pallas_call x4 -> x2, Pallas kernels: 11.8 us -> 6.29 us  [grads(): pl.pallas_call(functools.partial(grad_kernel, heads=2, groups=groups, **s...]
    pallas_call x4 -> x6, Pallas kernels: 2.67 us -> 5.28 us  [call(): pl.pallas_call(kernel, in_specs=[in_smem] + [in_vmem] * len(args) + [anyw...]
    ppermute x8, waiting for transfers between devices: 3.52 us -> 2.12 us  [swap_cores(): return lax.ppermute(a, 'seq', [(b, b ^ 1) for b in range(seq)])]
  transfers between devices with their start and end apart: 16 -> 16, of which waited for: 10 -> 7; matrix products, arithmetic and copies ran while one was open for 0% -> 0% of each run, Pallas kernels for 31% -> 38%
where the time goes in v1:
time: 66.6 us; the launch traced here: 66.2 us
  Pallas kernels  28.5 us (43%)
  starting transfers between devices  19.9 us (30%)
  waiting for transfers between devices  16.2 us (24%)
  between operations  0.88 us (1%)
  local copies, waits for them, and re-layouts  0.69 us (1%)
    ppermute x4, starting transfers between devices, swap_pairs(): came.append(lax.ppermute(sent, 'seq', perm + [(b, a) for a, b in perm]))  13.6 us
    ppermute x4, waiting for transfers between devices, send_rows(): lax.ppermute(outs[j], 'head', [(x, (x + j) % groups) for x in range(group...  11.1 us
    pallas_call x2, Pallas kernels, local(): pl.pallas_call(functools.partial(local_kernel, heads=2, **sizes), grid_sp...  8.16 us
    pallas_call x2, Pallas kernels, grads(): pl.pallas_call(functools.partial(grad_kernel, heads=2, groups=groups, **s...  6.29 us
    pallas_call x6, Pallas kernels, call(): pl.pallas_call(kernel, in_specs=[in_smem] + [in_vmem] * len(args) + [anyw...  5.28 us
    pallas_call x2, Pallas kernels, states(): pl.pallas_call(functools.partial(state_kernel, offset=offset, heads=heads...  5.12 us
    ppermute x4, starting transfers between devices, send_rows(): lax.ppermute(outs[j], 'head', [(x, (x + j) % groups) for x in range(group...  4.39 us
    pallas_call x4, Pallas kernels, shards(): pl.pallas_call(functools.partial(place_kernel, groups=groups, offset=offs...  3.7 us
  transfers between devices with their start and end apart: 16, of which 7 were waited for; matrix products, arithmetic and copies ran while one was open for 0% of the time, Pallas kernels for 38%

profile of v1, /device:TPU:0, one launch (start us, length us, event | category | flops | bytes accessed | tf_op | source)
XLA Modules:
  0.0 66.2 jit_solution(10096876784141044893)
XLA Ops:
  0.6 0.0 copy-start.6
  0.6 0.6 copy-done.6
  1.3 2.6 %states.2 = (f32[8,128,128]{2,1,0:T(8,128)S(1)}, f32[8,128,128]{2,1,0:T(8,128)S(1)}) custom-call(s32[8]{0:T(128)S(1)} %copy-done.6, bf16[256,2048]{1,0:T(8,128)(2,1)} %q.11, bf16[256,2048]{1,0:T(8,128)(2,1)} %k.11, bf16[256,2048]{1,0:T(8,128)(2,1)} %v.11, bf16[256,2048]{1,0:T(8,128)(2,1)} %g.11), custom_call_target="tpu_custom_call" | custom-call | bytes 1024 | tf_op jit(solution)/shard_map/states/pallas_call | solution.py:282
  3.9 0.5 collective-permute-start
  4.4 0.0 copy-start.7
  4.4 0.1 collective-permute-start.3
  4.5 4.1 %local.2 = (f32[3,256,512]{2,1,0:T(8,128)}, bf16[3,256,512]{2,1,0:T(8,128)(2,1)S(1)}, f32[8,128]{1,0:T(8,128)S(1)}) custom-call(s32[8]{0:T(128)S(1)} %copy-done.6, bf16[256,2048]{1,0:T(8,128)(2,1)} %q.11, bf16[256,2048]{1,0:T(8,128)(2,1)} %k.11, bf16[256,2048]{1,0:T(8,128)(2,1)} %v.11, bf16[256,2048]{1,0:T(8,128)(2,1)} %g.11, ...), custom_call_target="tpu_custom_call" | custom-call | bytes 1024 | tf_op jit(solution)/shard_map/local/pallas_call | solution.py:321
  8.5 0.0 collective-permute-done.got
  8.5 0.6 pair.2.rest_0_
  9.2 4.5 %collective-permute-start.4 = (bf16[8,128,128]{2,1,0:T(8,128)(2,1)S(1)}, bf16[8,128,128]{2,1,0:T(8,128)(2,1)S(1)}, u32[]{:S(2)}, u32[]{:S(2)}) collective-permute-start(bf16[8,128,128]{2,1,0:T(8,128)(2,1)S(1)} %pair.2.rest_0_), channel_id=1, source_target_pairs={{0,6},{4,10},{8,14},{12,18},{16,22},{20,26},{24,30},{6,0},{10,4},{... | collective-permute-start | bytes 786440 | tf_op jit(solution)/shard_map/ppermute | solution.py:268
  13.7 3.4 %collective-permute-start.5 = (bf16[8,128,128]{2,1,0:T(8,128)(2,1)S(1)}, bf16[8,128,128]{2,1,0:T(8,128)(2,1)S(1)}, u32[]{:S(2)}, u32[]{:S(2)}) collective-permute-start(bf16[8,128,128]{2,1,0:T(8,128)(2,1)S(1)} %pair.2.rest_0_), channel_id=1, source_target_pairs={{0,10},{4,14},{8,18},{12,22},{16,26},{20,30},{10,0},{14,4},{18,8},... | collective-permute-start | bytes 786440 | tf_op jit(solution)/shard_map/ppermute | solution.py:268
  17.1 0.0 copy-done.7
  17.1 2.6 %states.3 = (f32[8,128,128]{2,1,0:T(8,128)S(1)}, f32[8,128,128]{2,1,0:T(8,128)S(1)}) custom-call(s32[8]{0:T(128)S(1)} %copy-done.7, bf16[256,2048]{1,0:T(8,128)(2,1)} %q.11, bf16[256,2048]{1,0:T(8,128)(2,1)} %k.11, bf16[256,2048]{1,0:T(8,128)(2,1)} %v.11, bf16[256,2048]{1,0:T(8,128)(2,1)} %g.11, bf16[8,128,128]{2,1,0:T(8,128)(2,1)S(1)} %pair.2.rest_0_), custom_call_target="tpu_custom_call" | custom-call | bytes 1024 | tf_op jit(solution)/shard_map/states/pallas_call | solution.py:282
  19.7 0.1 collective-permute-start.2
  19.8 0.0 copy-start.4
  19.8 4.1 %local.3 = (f32[3,256,512]{2,1,0:T(8,128)}, bf16[3,256,512]{2,1,0:T(8,128)(2,1)S(1)}, f32[8,128]{1,0:T(8,128)S(1)}) custom-call(s32[8]{0:T(128)S(1)} %copy-done.7, bf16[256,2048]{1,0:T(8,128)(2,1)} %q.11, bf16[256,2048]{1,0:T(8,128)(2,1)} %k.11, bf16[256,2048]{1,0:T(8,128)(2,1)} %v.11, bf16[256,2048]{1,0:T(8,128)(2,1)} %g.11, ...), custom_call_target="tpu_custom_call" | custom-call | bytes 1024 | tf_op jit(solution)/shard_map/local/pallas_call | solution.py:321
  23.9 0.0 collective-permute-done.3.other
  23.9 0.0 collective-permute-done.4.rest_0_
  23.9 0.0 collective-permute-done.5.rest_1_
  23.9 0.7 %join.2 = (f32[4,128,128]{2,1,0:T(8,128)S(1)}, f32[4,128,128]{2,1,0:T(8,128)S(1)}, f32[4,128,128]{2,1,0:T(8,128)S(1)}, f32[4,128,128]{2,1,0:T(8,128)S(1)}) custom-call(s32[8]{0:T(128)S(1)} %copy-done.7, f32[8,128,128]{2,1,0:T(8,128)S(1)} %collective-permute-done.3.other, bf16[8,128,128]{2,1,0:T(8,128)(2,1)S(1)} %collective-permute-done.4.rest_0_, ...), custom_call_target="tpu_custom_call" | custom-call | bytes 1024 | tf_op jit(solution)/shard_map/join/pallas_call | solution.py:255
  24.6 0.5 collective-permute-start.6
  25.2 0.1 collective-permute-start.1
  25.2 1.1 %collective-permute-done.6.got = f32[4,128,128]{2,1,0:T(8,128)S(1)} collective-permute-done((f32[4,128,128]{2,1,0:T(8,128)S(1)}, f32[4,128,128]{2,1,0:T(8,128)S(1)}, u32[]{:S(2)}, u32[]{:S(2)}) %collective-permute-start.6) | collective-permute-done | bytes 262176 | tf_op jit(solution)/shard_map/ppermute | solution.py:262
  26.3 0.0 copy-done.4
  26.3 1.3 %carry.2 = (bf16[3,128,512]{2,1,0:T(8,128)(2,1)S(1)}, bf16[3,128,512]{2,1,0:T(8,128)(2,1)S(1)}) custom-call(s32[8]{0:T(128)S(1)} %copy-done.7, f32[3,256,512]{2,1,0:T(8,128)S(1)} %copy-done.4, bf16[3,256,512]{2,1,0:T(8,128)(2,1)S(1)} %get-tuple-element.44.kvg, f32[4,128,128]{2,1,0:T(8,128)S(1)} %get-tuple-element.46.mine, ...), custom_call_target="tpu_custom_call" | custom-call | bytes 1024 | tf_op jit(solution)/shard_map/carry/pallas_call | solution.py:255
  27.6 0.0 copy-start.5
  27.6 1.6 %collective-permute-start.9 = (bf16[3,128,512]{2,1,0:T(8,128)(2,1)S(1)}, bf16[3,128,512]{2,1,0:T(8,128)(2,1)S(1)}, u32[]{:S(2)}, u32[]{:S(2)}) collective-permute-start(bf16[3,128,512]{2,1,0:T(8,128)(2,1)S(1)} %get-tuple-element.49), channel_id=1, source_target_pairs={{0,1},{1,0},{2,3},{3,2},{4,5},{5,4},{6,7},{7,6},{8,9},{9,8},{10,11... | collective-permute-start | bytes 1179656 | tf_op jit(solution)/shard_map/ppermute | solution.py:274
  29.2 0.1 collective-permute-start.12
  29.3 0.0 collective-permute-done.2.got
  29.3 0.6 pair.3
  29.9 2.6 %collective-permute-start.7 = (bf16[8,128,128]{2,1,0:T(8,128)(2,1)S(1)}, bf16[8,128,128]{2,1,0:T(8,128)(2,1)S(1)}, u32[]{:S(2)}, u32[]{:S(2)}) collective-permute-start(bf16[8,128,128]{2,1,0:T(8,128)(2,1)S(1)} %pair.3), channel_id=1, source_target_pairs={{0,6},{4,10},{8,14},{12,18},{16,22},{20,26},{24,30},{6,0},{10,4},{... | collective-permute-start | bytes 786440 | tf_op jit(solution)/shard_map/ppermute | solution.py:268
  32.5 3.1 %collective-permute-start.8 = (bf16[8,128,128]{2,1,0:T(8,128)(2,1)S(1)}, bf16[8,128,128]{2,1,0:T(8,128)(2,1)S(1)}, u32[]{:S(2)}, u32[]{:S(2)}) collective-permute-start(bf16[8,128,128]{2,1,0:T(8,128)(2,1)S(1)} %pair.3), channel_id=1, source_target_pairs={{0,10},{4,14},{8,18},{12,22},{16,26},{20,30},{10,0},{14,4},{18,8},... | collective-permute-start | bytes 786440 | tf_op jit(solution)/shard_map/ppermute | solution.py:268
  35.5 0.0 collective-permute-done.12.got
  35.6 0.0 copy-done.5
  35.6 0.0 copy-start
  35.6 0.0 copy-start.1
  35.6 0.0 copy-start.2
  35.6 0.0 copy-start.3
  35.6 1.3 %carry.3 = (bf16[3,128,512]{2,1,0:T(8,128)(2,1)S(1)}, bf16[3,128,512]{2,1,0:T(8,128)(2,1)S(1)}) custom-call(s32[8]{0:T(128)S(1)} %copy-done.7, f32[3,256,512]{2,1,0:T(8,128)S(1)} %copy-done.5, bf16[3,256,512]{2,1,0:T(8,128)(2,1)S(1)} %get-tuple-element.55.kvg, f32[4,128,128]{2,1,0:T(8,128)S(1)} %get-tuple-element.56.mine, ...), custom_call_target="tpu_custom_call" | custom-call | bytes 1024 | tf_op jit(solution)/shard_map/carry/pallas_call | solution.py:255
  36.9 0.6 collective-permute-start.13
  37.5 0.0 collective-permute-done.1.other
  37.5 1.6 %collective-permute-done.7.rest_0_ = bf16[8,128,128]{2,1,0:T(8,128)(2,1)S(1)} collective-permute-done((bf16[8,128,128]{2,1,0:T(8,128)(2,1)S(1)}, bf16[8,128,128]{2,1,0:T(8,128)(2,1)S(1)}, u32[]{:S(2)}, u32[]{:S(2)}) %collective-permute-start.7) | collective-permute-done | bytes 262176 | tf_op jit(solution)/shard_map/ppermute | solution.py:268
  39.2 1.3 %collective-permute-done.8.rest_1_ = bf16[8,128,128]{2,1,0:T(8,128)(2,1)S(1)} collective-permute-done((bf16[8,128,128]{2,1,0:T(8,128)(2,1)S(1)}, bf16[8,128,128]{2,1,0:T(8,128)(2,1)S(1)}, u32[]{:S(2)}, u32[]{:S(2)}) %collective-permute-start.8) | collective-permute-done | bytes 262176 | tf_op jit(solution)/shard_map/ppermute | solution.py:268
  40.5 0.0 collective-permute-done.9.rest_2_.refs_1_
  40.5 0.7 %join.3 = (f32[4,128,128]{2,1,0:T(8,128)S(1)}, f32[4,128,128]{2,1,0:T(8,128)S(1)}, f32[4,128,128]{2,1,0:T(8,128)S(1)}, f32[4,128,128]{2,1,0:T(8,128)S(1)}) custom-call(s32[8]{0:T(128)S(1)} %copy-done.7, f32[8,128,128]{2,1,0:T(8,128)S(1)} %collective-permute-done.1.other, bf16[8,128,128]{2,1,0:T(8,128)(2,1)S(1)} %collective-permute-done.7.rest_0_, ...), custom_call_target="tpu_custom_call" | custom-call | bytes 1024 | tf_op jit(solution)/shard_map/join/pallas_call | solution.py:255
  41.2 0.1 collective-permute-start.11
  41.3 0.5 collective-permute-start.10
  41.8 1.0 %collective-permute-done.11.got = f32[4,128,128]{2,1,0:T(8,128)S(1)} collective-permute-done((f32[4,128,128]{2,1,0:T(8,128)S(1)}, f32[4,128,128]{2,1,0:T(8,128)S(1)}, u32[]{:S(2)}, u32[]{:S(2)}) %collective-permute-start.11) | collective-permute-done | bytes 262176 | tf_op jit(solution)/shard_map/ppermute | solution.py:262
  42.8 0.0 copy-done
  42.9 0.0 copy-done.1
  42.9 0.0 copy-done.2
  42.9 0.0 copy-done.3
  42.9 2.8 %grads.2 = (bf16[3,128,512]{2,1,0:T(8,128)(2,1)S(1)}, bf16[3,128,512]{2,1,0:T(8,128)(2,1)S(1)}) custom-call(s32[8]{0:T(128)S(1)} %copy-done.7, bf16[256,2048]{1,0:T(8,128)(2,1)S(1)} %copy-done, bf16[256,2048]{1,0:T(8,128)(2,1)S(1)} %copy-done.1, bf16[256,2048]{1,0:T(8,128)(2,1)S(1)} %copy-done.2, bf16[256,2048]{1,0:T(8,128)(2,1)S(1)} %copy-done.3, ...), custom_call_target="tpu_custom_call" | custom-call | bytes 1024 | tf_op jit(solution)/shard_map/grads/pallas_call | solution.py:307
  45.6 0.7 %collective-permute-start.15 = (bf16[3,128,512]{2,1,0:T(8,128)(2,1)S(1)}, bf16[3,128,512]{2,1,0:T(8,128)(2,1)S(1)}, u32[]{:S(2)}, u32[]{:S(2)}) collective-permute-start(bf16[3,128,512]{2,1,0:T(8,128)(2,1)S(1)} %get-tuple-element.63), channel_id=1, source_target_pairs={{0,1},{1,0},{2,3},{3,2},{4,5},{5,4},{6,7},{7,6},{8,9},{9,8},{10,11... | collective-permute-start | bytes 1179656 | tf_op jit(solution)/shard_map/ppermute | solution.py:274
  46.3 1.2 %collective-permute-done.13.rest_1_.refs_1_ = bf16[3,128,512]{2,1,0:T(8,128)(2,1)S(1)} collective-permute-done((bf16[3,128,512]{2,1,0:T(8,128)(2,1)S(1)}, bf16[3,128,512]{2,1,0:T(8,128)(2,1)S(1)}, u32[]{:S(2)}, u32[]{:S(2)}) %collective-permute-start.13) | collective-permute-done | bytes 393248 | tf_op jit(solution)/shard_map/ppermute | solution.py:274
  47.5 0.0 collective-permute-done.10.got
  47.5 3.5 %grads.3 = (bf16[3,128,512]{2,1,0:T(8,128)(2,1)S(1)}, bf16[3,128,512]{2,1,0:T(8,128)(2,1)S(1)}) custom-call(s32[8]{0:T(128)S(1)} %copy-done.7, bf16[256,2048]{1,0:T(8,128)(2,1)S(1)} %copy-done, bf16[256,2048]{1,0:T(8,128)(2,1)S(1)} %copy-done.1, bf16[256,2048]{1,0:T(8,128)(2,1)S(1)} %copy-done.2, bf16[256,2048]{1,0:T(8,128)(2,1)} %g.11, ...), custom_call_target="tpu_custom_call" | custom-call | bytes 1024 | tf_op jit(solution)/shard_map/grads/pallas_call | solution.py:307
  51.1 1.6 %collective-permute-start.14 = (bf16[3,128,512]{2,1,0:T(8,128)(2,1)S(1)}, bf16[3,128,512]{2,1,0:T(8,128)(2,1)S(1)}, u32[]{:S(2)}, u32[]{:S(2)}) collective-permute-start(bf16[3,128,512]{2,1,0:T(8,128)(2,1)S(1)} %get-tuple-element.62), channel_id=1, source_target_pairs={{0,1},{1,0},{2,3},{3,2},{4,5},{5,4},{6,7},{7,6},{8,9},{9,8},{10,11... | collective-permute-start | bytes 1179656 | tf_op jit(solution)/shard_map/ppermute | solution.py:274
  52.6 0.9 %place.4 = (bf16[128,4096]{1,0:T(8,128)(2,1)}, bf16[128,4096]{1,0:T(8,128)(2,1)}, bf16[128,4096]{1,0:T(8,128)(2,1)}) custom-call(bf16[3,128,512]{2,1,0:T(8,128)(2,1)S(1)} %get-tuple-element.48.rest_0_.refs_0_, bf16[3,128,512]{2,1,0:T(8,128)(2,1)S(1)} %collective-permute-done.9.rest_2_.refs_1_), custom_call_target="tpu_custom_call" | custom-call | bytes 1024 | tf_op jit(solution)/shard_map/place/pallas_call | solution.py:361
  53.5 0.9 %place.5 = (bf16[128,4096]{1,0:T(8,128)(2,1)}, bf16[128,4096]{1,0:T(8,128)(2,1)}, bf16[128,4096]{1,0:T(8,128)(2,1)}) custom-call(bf16[3,128,512]{2,1,0:T(8,128)(2,1)S(1)} %get-tuple-element.58.rest_0_.refs_0_, bf16[3,128,512]{2,1,0:T(8,128)(2,1)S(1)} %collective-permute-done.13.rest_1_.refs_1_, ...), custom_call_target="tpu_custom_call", output_to_operand_aliasing={{0}: (2, {}), {1}: (3, {}), {2}: (4, {})} | custom-call | bytes 1024 | tf_op jit(solution)/shard_map/place/pallas_call | solution.py:361
  54.5 3.2 %collective-permute-done.15.refs_1_ = bf16[3,128,512]{2,1,0:T(8,128)(2,1)S(1)} collective-permute-done((bf16[3,128,512]{2,1,0:T(8,128)(2,1)S(1)}, bf16[3,128,512]{2,1,0:T(8,128)(2,1)S(1)}, u32[]{:S(2)}, u32[]{:S(2)}) %collective-permute-start.15) | collective-permute-done | bytes 393248 | tf_op jit(solution)/shard_map/ppermute | solution.py:274
  57.7 0.9 %place.6 = (bf16[128,4096]{1,0:T(8,128)(2,1)}, bf16[128,4096]{1,0:T(8,128)(2,1)}, bf16[128,4096]{1,0:T(8,128)(2,1)}) custom-call(bf16[3,128,512]{2,1,0:T(8,128)(2,1)S(1)} %get-tuple-element.59.rest_0_.refs_0_, bf16[3,128,512]{2,1,0:T(8,128)(2,1)S(1)} %collective-permute-done.15.refs_1_, ...), custom_call_target="tpu_custom_call", output_to_operand_aliasing={{0}: (2, {}), {1}: (3, {}), {2}: (4, {})} | custom-call | bytes 1024 | tf_op jit(solution)/shard_map/place/pallas_call | solution.py:361
  58.6 6.7 %collective-permute-done.14.refs_1_ = bf16[3,128,512]{2,1,0:T(8,128)(2,1)S(1)} collective-permute-done((bf16[3,128,512]{2,1,0:T(8,128)(2,1)S(1)}, bf16[3,128,512]{2,1,0:T(8,128)(2,1)S(1)}, u32[]{:S(2)}, u32[]{:S(2)}) %collective-permute-start.14) | collective-permute-done | bytes 393248 | tf_op jit(solution)/shard_map/ppermute | solution.py:274
  65.3 0.9 %place.7 = (bf16[128,4096]{1,0:T(8,128)(2,1)}, bf16[128,4096]{1,0:T(8,128)(2,1)}, bf16[128,4096]{1,0:T(8,128)(2,1)}) custom-call(bf16[3,128,512]{2,1,0:T(8,128)(2,1)S(1)} %get-tuple-element.61.refs_0_, bf16[3,128,512]{2,1,0:T(8,128)(2,1)S(1)} %collective-permute-done.14.refs_1_, ...), custom_call_target="tpu_custom_call", output_to_operand_aliasing={{0}: (2, {}), {1}: (3, {}), {2}: (4, {})} | custom-call | bytes 1024 | tf_op jit(solution)/shard_map/place/pallas_call | solution.py:361
Async XLA Ops:
  0.6 0.7 copy-start.6
  3.9 4.7 %collective-permute-start = (f32[8,128,128]{2,1,0:T(8,128)S(1)}, f32[8,128,128]{2,1,0:T(8,128)S(1)}, u32[]{:S(2)}, u32[]{:S(2)}) collective-permute-start(f32[8,128,128]{2,1,0:T(8,128)S(1)} %get-tuple-element.39), channel_id=1, source_target_pairs={{0,2},{2,0},{4,6},{6,4},{8,10},{10,8},{12,14},{14,12},{16,18},{18,... | collective-permute-start | bytes 1572872 | tf_op jit(solution)/shard_map/ppermute | solution.py:262
  4.4 12.7 %copy-start.7 = (s32[8]{0:T(128)S(1)}, s32[8]{0:T(128)}, u32[]{:S(2)}) copy-start(s32[8]{0:T(128)} %lengths.23) | copy-start | bytes 100
  4.4 19.5 %collective-permute-start.3 = (f32[8,128,128]{2,1,0:T(8,128)S(1)}, f32[8,128,128]{2,1,0:T(8,128)S(1)}, u32[]{:S(2)}, u32[]{:S(2)}) collective-permute-start(f32[8,128,128]{2,1,0:T(8,128)S(1)} %get-tuple-element.38.rest_0_.kept), channel_id=1, source_target_pairs={{0,2},{2,0},{4,6},{6,4},{8,10},{10,8},{12,14},{14,12},{16,18},{18,... | collective-permute-start | bytes 1572872 | tf_op jit(solution)/shard_map/ppermute | solution.py:262
  9.2 14.7 %collective-permute-start.4 = (bf16[8,128,128]{2,1,0:T(8,128)(2,1)S(1)}, bf16[8,128,128]{2,1,0:T(8,128)(2,1)S(1)}, u32[]{:S(2)}, u32[]{:S(2)}) collective-permute-start(bf16[8,128,128]{2,1,0:T(8,128)(2,1)S(1)} %pair.2.rest_0_), channel_id=1, source_target_pairs={{0,6},{4,10},{8,14},{12,18},{16,22},{20,26},{24,30},{6,0},{10,4},{... | collective-permute-start | bytes 786440 | tf_op jit(solution)/shard_map/ppermute | solution.py:268
  13.7 10.2 %collective-permute-start.5 = (bf16[8,128,128]{2,1,0:T(8,128)(2,1)S(1)}, bf16[8,128,128]{2,1,0:T(8,128)(2,1)S(1)}, u32[]{:S(2)}, u32[]{:S(2)}) collective-permute-start(bf16[8,128,128]{2,1,0:T(8,128)(2,1)S(1)} %pair.2.rest_0_), channel_id=1, source_target_pairs={{0,10},{4,14},{8,18},{12,22},{16,26},{20,30},{10,0},{14,4},{18,8},... | collective-permute-start | bytes 786440 | tf_op jit(solution)/shard_map/ppermute | solution.py:268
  19.7 9.6 %collective-permute-start.2 = (f32[8,128,128]{2,1,0:T(8,128)S(1)}, f32[8,128,128]{2,1,0:T(8,128)S(1)}, u32[]{:S(2)}, u32[]{:S(2)}) collective-permute-start(f32[8,128,128]{2,1,0:T(8,128)S(1)} %get-tuple-element.42), channel_id=1, source_target_pairs={{0,2},{2,0},{4,6},{6,4},{8,10},{10,8},{12,14},{14,12},{16,18},{18,... | collective-permute-start | bytes 1572872 | tf_op jit(solution)/shard_map/ppermute | solution.py:262
  19.8 6.6 %copy-start.4 = (f32[3,256,512]{2,1,0:T(8,128)S(1)}, f32[3,256,512]{2,1,0:T(8,128)}, u32[]{:S(2)}) copy-start(f32[3,256,512]{2,1,0:T(8,128)} %get-tuple-element.43.near) | copy-start | bytes 4718596
  24.6 1.7 %collective-permute-start.6 = (f32[4,128,128]{2,1,0:T(8,128)S(1)}, f32[4,128,128]{2,1,0:T(8,128)S(1)}, u32[]{:S(2)}, u32[]{:S(2)}) collective-permute-start(f32[4,128,128]{2,1,0:T(8,128)S(1)} %get-tuple-element.47), channel_id=1, source_target_pairs={{0,2},{2,0},{4,6},{6,4},{8,10},{10,8},{12,14},{14,12},{16,18},{18,... | collective-permute-start | bytes 786440 | tf_op jit(solution)/shard_map/ppermute | solution.py:262
  25.2 12.4 %collective-permute-start.1 = (f32[8,128,128]{2,1,0:T(8,128)S(1)}, f32[8,128,128]{2,1,0:T(8,128)S(1)}, u32[]{:S(2)}, u32[]{:S(2)}) collective-permute-start(f32[8,128,128]{2,1,0:T(8,128)S(1)} %get-tuple-element.41.kept), channel_id=1, source_target_pairs={{0,2},{2,0},{4,6},{6,4},{8,10},{10,8},{12,14},{14,12},{16,18},{18,... | collective-permute-start | bytes 1572872 | tf_op jit(solution)/shard_map/ppermute | solution.py:262
  27.6 7.9 %copy-start.5 = (f32[3,256,512]{2,1,0:T(8,128)S(1)}, f32[3,256,512]{2,1,0:T(8,128)}, u32[]{:S(2)}) copy-start(f32[3,256,512]{2,1,0:T(8,128)} %get-tuple-element.54.near) | copy-start | bytes 4718596
  27.6 12.9 %collective-permute-start.9 = (bf16[3,128,512]{2,1,0:T(8,128)(2,1)S(1)}, bf16[3,128,512]{2,1,0:T(8,128)(2,1)S(1)}, u32[]{:S(2)}, u32[]{:S(2)}) collective-permute-start(bf16[3,128,512]{2,1,0:T(8,128)(2,1)S(1)} %get-tuple-element.49), channel_id=1, source_target_pairs={{0,1},{1,0},{2,3},{3,2},{4,5},{5,4},{6,7},{7,6},{8,9},{9,8},{10,11... | collective-permute-start | bytes 1179656 | tf_op jit(solution)/shard_map/ppermute | solution.py:274
  29.2 6.4 %collective-permute-start.12 = (f32[4,128,128]{2,1,0:T(8,128)S(1)}, f32[4,128,128]{2,1,0:T(8,128)S(1)}, u32[]{:S(2)}, u32[]{:S(2)}) collective-permute-start(f32[4,128,128]{2,1,0:T(8,128)S(1)} %get-tuple-element.57), channel_id=1, source_target_pairs={{0,2},{2,0},{4,6},{6,4},{8,10},{10,8},{12,14},{14,12},{16,18},{18,... | collective-permute-start | bytes 786440 | tf_op jit(solution)/shard_map/ppermute | solution.py:262
  29.9 9.3 %collective-permute-start.7 = (bf16[8,128,128]{2,1,0:T(8,128)(2,1)S(1)}, bf16[8,128,128]{2,1,0:T(8,128)(2,1)S(1)}, u32[]{:S(2)}, u32[]{:S(2)}) collective-permute-start(bf16[8,128,128]{2,1,0:T(8,128)(2,1)S(1)} %pair.3), channel_id=1, source_target_pairs={{0,6},{4,10},{8,14},{12,18},{16,22},{20,26},{24,30},{6,0},{10,4},{... | collective-permute-start | bytes 786440 | tf_op jit(solution)/shard_map/ppermute | solution.py:268
  32.5 8.0 %collective-permute-start.8 = (bf16[8,128,128]{2,1,0:T(8,128)(2,1)S(1)}, bf16[8,128,128]{2,1,0:T(8,128)(2,1)S(1)}, u32[]{:S(2)}, u32[]{:S(2)}) collective-permute-start(bf16[8,128,128]{2,1,0:T(8,128)(2,1)S(1)} %pair.3), channel_id=1, source_target_pairs={{0,10},{4,14},{8,18},{12,22},{16,26},{20,30},{10,0},{14,4},{18,8},... | collective-permute-start | bytes 786440 | tf_op jit(solution)/shard_map/ppermute | solution.py:268
  35.6 7.3 %copy-start = (bf16[256,2048]{1,0:T(8,128)(2,1)S(1)}, bf16[256,2048]{1,0:T(8,128)(2,1)}, u32[]{:S(2)}) copy-start(bf16[256,2048]{1,0:T(8,128)(2,1)} %q.11) | copy-start | bytes 3145732
  35.6 7.3 %copy-start.1 = (bf16[256,2048]{1,0:T(8,128)(2,1)S(1)}, bf16[256,2048]{1,0:T(8,128)(2,1)}, u32[]{:S(2)}) copy-start(bf16[256,2048]{1,0:T(8,128)(2,1)} %k.11) | copy-start | bytes 3145732
  35.6 7.3 %copy-start.2 = (bf16[256,2048]{1,0:T(8,128)(2,1)S(1)}, bf16[256,2048]{1,0:T(8,128)(2,1)}, u32[]{:S(2)}) copy-start(bf16[256,2048]{1,0:T(8,128)(2,1)} %v.11) | copy-start | bytes 3145732
  35.6 7.3 %copy-start.3 = (bf16[256,2048]{1,0:T(8,128)(2,1)S(1)}, bf16[256,2048]{1,0:T(8,128)(2,1)}, u32[]{:S(2)}) copy-start(bf16[256,2048]{1,0:T(8,128)(2,1)} %g.11) | copy-start | bytes 3145732
  36.9 10.6 %collective-permute-start.13 = (bf16[3,128,512]{2,1,0:T(8,128)(2,1)S(1)}, bf16[3,128,512]{2,1,0:T(8,128)(2,1)S(1)}, u32[]{:S(2)}, u32[]{:S(2)}) collective-permute-start(bf16[3,128,512]{2,1,0:T(8,128)(2,1)S(1)} %get-tuple-element.60), channel_id=1, source_target_pairs={{0,1},{1,0},{2,3},{3,2},{4,5},{5,4},{6,7},{7,6},{8,9},{9,8},{10,11... | collective-permute-start | bytes 1179656 | tf_op jit(solution)/shard_map/ppermute | solution.py:274
  41.2 1.6 %collective-permute-start.11 = (f32[4,128,128]{2,1,0:T(8,128)S(1)}, f32[4,128,128]{2,1,0:T(8,128)S(1)}, u32[]{:S(2)}, u32[]{:S(2)}) collective-permute-start(f32[4,128,128]{2,1,0:T(8,128)S(1)} %get-tuple-element.53), channel_id=1, source_target_pairs={{0,2},{2,0},{4,6},{6,4},{8,10},{10,8},{12,14},{14,12},{16,18},{18,... | collective-permute-start | bytes 786440 | tf_op jit(solution)/shard_map/ppermute | solution.py:262
  41.3 6.2 %collective-permute-start.10 = (f32[4,128,128]{2,1,0:T(8,128)S(1)}, f32[4,128,128]{2,1,0:T(8,128)S(1)}, u32[]{:S(2)}, u32[]{:S(2)}) collective-permute-start(f32[4,128,128]{2,1,0:T(8,128)S(1)} %get-tuple-element.51), channel_id=1, source_target_pairs={{0,2},{2,0},{4,6},{6,4},{8,10},{10,8},{12,14},{14,12},{16,18},{18,... | collective-permute-start | bytes 786440 | tf_op jit(solution)/shard_map/ppermute | solution.py:262
  45.6 12.0 %collective-permute-start.15 = (bf16[3,128,512]{2,1,0:T(8,128)(2,1)S(1)}, bf16[3,128,512]{2,1,0:T(8,128)(2,1)S(1)}, u32[]{:S(2)}, u32[]{:S(2)}) collective-permute-start(bf16[3,128,512]{2,1,0:T(8,128)(2,1)S(1)} %get-tuple-element.63), channel_id=1, source_target_pairs={{0,1},{1,0},{2,3},{3,2},{4,5},{5,4},{6,7},{7,6},{8,9},{9,8},{10,11... | collective-permute-start | bytes 1179656 | tf_op jit(solution)/shard_map/ppermute | solution.py:274
  51.1 14.2 %collective-permute-start.14 = (bf16[3,128,512]{2,1,0:T(8,128)(2,1)S(1)}, bf16[3,128,512]{2,1,0:T(8,128)(2,1)S(1)}, u32[]{:S(2)}, u32[]{:S(2)}) collective-permute-start(bf16[3,128,512]{2,1,0:T(8,128)(2,1)S(1)} %get-tuple-element.62), channel_id=1, source_target_pairs={{0,1},{1,0},{2,3},{3,2},{4,5},{5,4},{6,7},{7,6},{8,9},{9,8},{10,11... | collective-permute-start | bytes 1179656 | tf_op jit(solution)/shard_map/ppermute | solution.py:274

commit v2 on v0

--- a/solution.py
+++ b/solution.py
@@ -13,7 +13,7 @@
 CHUNK = 4
 LINK = jnp.bfloat16
 VMEM_LIMIT = 16 * 1024 * 1024
-GRAD_LIMIT = 48 * 1024 * 1024
+GRAD_LIMIT = 40 * 1024 * 1024
 FIRST_LIMIT = 52 * 1024 * 1024
 NT = (((1,), (1,)), ((), ()))
 TN = (((0,), (0,)), ((), ()))
@@ -115,39 +115,37 @@
     return jnp.concatenate([high, (a - high.astype(jnp.float32)).astype(jnp.bfloat16)], axis=axis)
 
 
-def grad_kernel(lengths, q, k, v, g, mine, got, *rest, ndocs, rows, heads, groups):
-    outs, lower, upper, done = rest[-3 - groups:-3], rest[-3], rest[-2], rest[-1]
+def mask_kernel(lengths, *rest, ndocs, rows):
+    lower, upper = rest[-2:]
+    line = lax.broadcasted_iota(jnp.int32, (rows, rows), 0)
+    across = lax.broadcasted_iota(jnp.int32, (rows, rows), 1)
+    begin_line = jnp.zeros((rows, rows), jnp.int32)
+    begin_across = jnp.zeros((rows, rows), jnp.int32)
+    start = jnp.int32(0) - lax.axis_index("seq") * rows
+    for i in range(ndocs):
+        begin_line = jnp.where(line >= start, start, begin_line)
+        begin_across = jnp.where(across >= start, start, begin_across)
+        start = start + lengths[i]
+    lower[...] = jnp.where((across <= line) & (across >= begin_line), 1.0, 0.0)
+    upper[...] = jnp.where((line <= across) & (line >= begin_across), 1.0, 0.0)
+
+
+def grad_kernel(lengths, q, k, v, g, lower, upper, mine, got, *rest, ndocs, rows, offset, heads, groups):
+    outs, done = rest[-1 - groups:-1], rest[-1]
     place, column = lax.axis_index("seq"), lax.axis_index("head")
-    base = place * rows
-
-    @pl.when(pl.program_id(0) == 0)
-    def _():
-        line = lax.broadcasted_iota(jnp.int32, (rows, rows), 0)
-        across = lax.broadcasted_iota(jnp.int32, (rows, rows), 1)
-        begin_line = jnp.zeros((rows, rows), jnp.int32)
-        begin_across = jnp.zeros((rows, rows), jnp.int32)
-        start = jnp.int32(0) - base
-        for i in range(ndocs):
-            begin_line = jnp.where(line >= start, start, begin_line)
-            begin_across = jnp.where(across >= start, start, begin_across)
-            start = start + lengths[i]
-        lower[...] = jnp.where((across <= line) & (across >= begin_line), 1, 0)
-        upper[...] = jnp.where((line <= across) & (line >= begin_across), 1, 0)
-
-    first_core = lax.rem(place, 2) == 0
-    _, _, _, _, first, last = block_range(lengths, ndocs, base, rows)
+    first_core = lax.rem(place, 2) == 0
+    _, _, _, _, first, last = block_range(lengths, ndocs, place * rows, rows)
     order = lax.broadcasted_iota(jnp.int32, (rows, HEAD_DIM), 0)
     first_rows, last_rows = order < first, order >= last
-    in_lower, in_upper = lower[...] == 1, upper[...] == 1
     for h in range(heads):
         cols = slice(h * HEAD_DIM, (h + 1) * HEAD_DIM)
         state = jnp.where(first_core, got[h], mine[h])
         grad = jnp.where(first_core, mine[h], got[h])
-        qh, kh, vh, gh = (ref[:, cols] for ref in (q, k, v, g))
+        qh, kh, vh, gh = (ref[:, offset + h * HEAD_DIM:offset + (h + 1) * HEAD_DIM] for ref in (q, k, v, g))
         k2, v2, g2 = (jnp.concatenate([a, a], axis=1) for a in (kh, vh, gh))
-        weight_gv = jnp.where(in_lower, dot(gh, vh, NT), 0.0).astype(jnp.bfloat16)
-        weight_vg = jnp.where(in_upper, dot(vh, gh, NT), 0.0).astype(jnp.bfloat16)
-        weight_kq = jnp.where(in_upper, dot(kh, qh, NT), 0.0).astype(jnp.bfloat16)
+        weight_gv = (dot(gh, vh, NT) * lower[...]).astype(jnp.bfloat16)
+        weight_vg = (dot(vh, gh, NT) * upper[...]).astype(jnp.bfloat16)
+        weight_kq = (dot(kh, qh, NT) * upper[...]).astype(jnp.bfloat16)
         carry_q = jnp.where(first_rows, dot(g2, split(state, 1), NT), 0.0)
         carry_k = jnp.where(last_rows, dot(v2, split(grad, 1), NT), 0.0)
         carry_v = jnp.where(last_rows, dot(k2, split(grad, 0), NN), 0.0)
@@ -188,7 +186,6 @@
     pairs = seq // 2
     hops = -(-MOST // (2 * rows))
     halves = cuts_of(width)
-    step = 2 * HEAD_DIM
     part = rows // groups
     anywhere = pl.BlockSpec(memory_space=pl.ANY)
     in_vmem = pl.BlockSpec(memory_space=pltpu.VMEM)
@@ -201,11 +198,11 @@
     def shape_of(*dims, dtype=f32):
         return jax.ShapeDtypeStruct(dims, dtype)
 
-    def call(name, kernel, args, outs, scratch=(), after=()):
+    def call(name, kernel, args, outs, scratch=(), after=(), limit=VMEM_LIMIT):
         return pl.pallas_call(
             kernel, in_specs=[in_smem] + [in_vmem] * len(args) + [anywhere] * len(after), out_specs=[in_vmem] * len(outs), out_shape=outs,
             scratch_shapes=list(scratch), cost_estimate=cheap,
-            compiler_params=pltpu.CompilerParams(vmem_limit_bytes=VMEM_LIMIT), name=name,
+            compiler_params=pltpu.CompilerParams(vmem_limit_bytes=limit), name=name,
         )(doc_lengths, *args, *after)
 
     def swap_cores(a):
@@ -236,11 +233,12 @@
             scratch_shapes=[pltpu.VMEM((4, rows, half), bf16), pltpu.SemaphoreType.DMA((heads // group, 4))],
             cost_estimate=cheap, compiler_params=pltpu.CompilerParams(vmem_limit_bytes=FIRST_LIMIT), name="states",
         )(doc_lengths, *inputs, *after)
-        return kept, swap_cores(sent)
+        return kept, sent
 
     def pair_up(kept, got, after):
         out = shape_of(*kept.shape, dtype=LINK)
-        return swap_pairs(call("pair", functools.partial(pair_kernel, **sizes), (kept, got), [out], after=after)[0])
+        total = call("pair", functools.partial(pair_kernel, **sizes), (kept, got), [out], after=after)[0]
+        return total, swap_pairs(total)
 
     def join(kept, came, chunks, after):
         counts = [cw // HEAD_DIM for _, cw in chunks]
@@ -250,30 +248,24 @@
         )
         return [(mine, swap_cores(theirs)) for mine, theirs in zip(joined[:len(chunks)], joined[len(chunks):])]
 
-    def grads(offset, cw, mine, theirs, after):
-        block = pl.BlockSpec((rows, step), lambda s, lengths: (0, offset // step + s))
-        state_block = pl.BlockSpec((2,) + square, lambda s, lengths: (s, 0, 0))
-        out_block = pl.BlockSpec((3, part, step), lambda s, lengths: (0, 0, s))
-        return pl.pallas_call(
-            functools.partial(grad_kernel, heads=2, groups=groups, **sizes),
-            grid_spec=pltpu.PrefetchScalarGridSpec(
-                num_scalar_prefetch=1, grid=(cw // step,),
-                in_specs=[block] * 4 + [state_block] * 2 + [anywhere] * len(after), out_specs=[out_block] * groups,
-                scratch_shapes=[pltpu.VMEM((rows, rows), jnp.int32)] * 2 + [pltpu.VMEM((3, rows, step), bf16)],
-            ),
-            out_shape=[shape_of(3, part, cw, dtype=bf16)] * groups, cost_estimate=cheap,
-            compiler_params=pltpu.CompilerParams(vmem_limit_bytes=GRAD_LIMIT), name="grads",
-        )(doc_lengths, *inputs, mine, theirs, *after)
-
-    own = []
-    for offset, half, _ in halves:
-        own.append(states(offset, half, [kept for kept, _ in own[-1:]]))
-    cuts, sent, arrived = [], [], []
-    for (kept, got), (_, _, chunks) in zip(own, halves):
-        came = pair_up(kept, got, [outs[0] for outs in sent[:1]])
-        for (offset, cw), (mine, theirs) in zip(chunks, join(kept, came, chunks, [parts[1] for parts in arrived[:1]])):
-            sent.append(grads(offset, cw, mine, theirs, [outs[0] for outs in sent[-1:]] + [parts[1] for parts in arrived[1:-1]][-1:]))
-            arrived.append(send_rows(sent[-1]))
+    def grads(masks, offset, cw, mine, theirs, after):
+        return call(
+            "grads", functools.partial(grad_kernel, offset=offset, heads=cw // HEAD_DIM, groups=groups, **sizes),
+            (*inputs, *masks, mine, theirs), [shape_of(3, part, cw, dtype=bf16)] * groups,
+            [pltpu.VMEM((3, rows, cw), bf16)], after, GRAD_LIMIT,
+        )
+
+    cuts, outs, arrived, totals, masks = [], [], [], [], None
+    for start, half, chunks in halves:
+        kept, sent = states(start, half, totals)
+        total, came = pair_up(kept, swap_cores(sent), [made[0] for made in outs[-1:]])
+        totals = [total]
+        masks = masks or call("masks", functools.partial(mask_kernel, **sizes), (), [shape_of(rows, rows)] * 2, after=totals)
+        joined = join(kept, came, chunks, [parts[1] for parts in arrived[:1]] or masks[:1])
+        for (offset, cw), (mine, theirs) in zip(chunks, joined):
+            after = [made[0] for made in outs[-1:]] + [parts[1] for parts in arrived[1:-1]][-1:]
+            outs.append(grads(masks, offset, cw, mine, theirs, after))
+            arrived.append(send_rows(outs[-1]))
         cuts += chunks
 
     placed = []

time: 64.2 us -> 64.5 us (level)
  waiting for transfers between devices: 18.2 us -> 21.6 us
  Pallas kernels: 23.6 us -> 21.1 us
  local copies, waits for them, and re-layouts: 1.33 us -> 0.67 us
    pallas_call x4 -> x0, Pallas kernels: 11.8 us -> none  [grads(): pl.pallas_call(functools.partial(grad_kernel, heads=2, groups=groups, **s...]
    pallas_call x4 -> x9, Pallas kernels: 2.67 us -> 12 us  [call(): pl.pallas_call(kernel, in_specs=[in_smem] + [in_vmem] * len(args) + [anyw...]
    ppermute x4, waiting for transfers between devices: 3.56 us -> 5.65 us  [swap_pairs(): came.append(lax.ppermute(sent, 'seq', perm + [(b, a) for a, b in perm]))]
    ppermute x4, waiting for transfers between devices: 11.1 us -> 12.5 us  [send_rows(): lax.ppermute(outs[j], 'head', [(x, (x + j) % groups) for x in range(group...]
    unnamed x12 -> x10, local copies, waits for them, and re-layouts: 1.33 us -> 0.67 us
  transfers between devices with their start and end apart: 16 -> 16, of which waited for: 10 -> 8; matrix products, arithmetic and copies ran while one was open for 0% -> 0% of each run, Pallas kernels for 31% -> 27%
where the time goes in v2:
time: 64.5 us; the launch traced here: 64.2 us
  waiting for transfers between devices  21.6 us (33%)
  Pallas kernels  21.1 us (33%)
  starting transfers between devices  20 us (31%)
  between operations  0.86 us (1%)
  local copies, waits for them, and re-layouts  0.67 us (1%)
    ppermute x4, starting transfers between devices, swap_pairs(): came.append(lax.ppermute(sent, 'seq', perm + [(b, a) for a, b in perm]))  13.8 us
    ppermute x4, waiting for transfers between devices, send_rows(): lax.ppermute(outs[j], 'head', [(x, (x + j) % groups) for x in range(group...  12.5 us
    pallas_call x9, Pallas kernels, call(): pl.pallas_call(kernel, in_specs=[in_smem] + [in_vmem] * len(args) + [anyw...  12 us
    ppermute x4, waiting for transfers between devices, swap_pairs(): came.append(lax.ppermute(sent, 'seq', perm + [(b, a) for a, b in perm]))  5.65 us
    pallas_call x2, Pallas kernels, states(): pl.pallas_call(functools.partial(state_kernel, offset=offset, heads=heads...  5.4 us
    ppermute x4, starting transfers between devices, send_rows(): lax.ppermute(outs[j], 'head', [(x, (x + j) % groups) for x in range(group...  4.34 us
    pallas_call x4, Pallas kernels, shards(): pl.pallas_call(functools.partial(place_kernel, groups=groups, offset=offs...  3.7 us
    ppermute x8, waiting for transfers between devices, swap_cores(): return lax.ppermute(a, 'seq', [(b, b ^ 1) for b in range(seq)])  3.44 us
  transfers between devices with their start and end apart: 16, of which 8 were waited for; matrix products, arithmetic and copies ran while one was open for 0% of the time, Pallas kernels for 27%

profile of v2, /device:TPU:0, one launch (start us, length us, event | category | flops | bytes accessed | tf_op | source)
XLA Modules:
  0.0 64.2 jit_solution(6456971764575300611)
XLA Ops:
  0.6 0.0 copy-start.4
  0.6 0.6 %copy-done.4 = s32[8]{0:T(128)S(1)} copy-done((s32[8]{0:T(128)S(1)}, s32[8]{0:T(128)}, u32[]{:S(2)}) %copy-start.4) | copy-done | bytes 56
  1.3 2.6 %states.2 = (f32[8,128,128]{2,1,0:T(8,128)S(1)}, f32[8,128,128]{2,1,0:T(8,128)S(1)}) custom-call(s32[8]{0:T(128)S(1)} %copy-done.4, bf16[256,2048]{1,0:T(8,128)(2,1)} %q.11, bf16[256,2048]{1,0:T(8,128)(2,1)} %k.11, bf16[256,2048]{1,0:T(8,128)(2,1)} %v.11, bf16[256,2048]{1,0:T(8,128)(2,1)} %g.11), custom_call_target="tpu_custom_call" | custom-call | bytes 1024 | tf_op jit(solution)/shard_map/states/pallas_call | solution.py:229
  3.9 0.5 collective-permute-start
  4.4 0.1 collective-permute-start.3
  4.4 1.5 %collective-permute-done.got = f32[8,128,128]{2,1,0:T(8,128)S(1)} collective-permute-done((f32[8,128,128]{2,1,0:T(8,128)S(1)}, f32[8,128,128]{2,1,0:T(8,128)S(1)}, u32[]{:S(2)}, u32[]{:S(2)}) %collective-permute-start) | collective-permute-done | bytes 524320 | tf_op jit(solution)/shard_map/ppermute | solution.py:209
  5.9 0.6 pair.2.rest_0_
  6.5 4.5 %collective-permute-start.4 = (bf16[8,128,128]{2,1,0:T(8,128)(2,1)S(1)}, bf16[8,128,128]{2,1,0:T(8,128)(2,1)S(1)}, u32[]{:S(2)}, u32[]{:S(2)}) collective-permute-start(bf16[8,128,128]{2,1,0:T(8,128)(2,1)S(1)} %pair.2.rest_0_), channel_id=1, source_target_pairs={{0,6},{4,10},{8,14},{12,18},{16,22},{20,26},{24,30},{6,0},{10,4},{... | collective-permute-start | bytes 786440 | tf_op jit(solution)/shard_map/ppermute | solution.py:215
  11.1 3.3 %collective-permute-start.5 = (bf16[8,128,128]{2,1,0:T(8,128)(2,1)S(1)}, bf16[8,128,128]{2,1,0:T(8,128)(2,1)S(1)}, u32[]{:S(2)}, u32[]{:S(2)}) collective-permute-start(bf16[8,128,128]{2,1,0:T(8,128)(2,1)S(1)} %pair.2.rest_0_), channel_id=1, source_target_pairs={{0,10},{4,14},{8,18},{12,22},{16,26},{20,30},{10,0},{14,4},{18,8},... | collective-permute-start | bytes 786440 | tf_op jit(solution)/shard_map/ppermute | solution.py:215
  14.4 0.0 copy-start.1
  14.4 0.0 copy-start.2
  14.5 0.0 copy-start.3
  14.5 2.8 %states.3 = (f32[8,128,128]{2,1,0:T(8,128)S(1)}, f32[8,128,128]{2,1,0:T(8,128)S(1)}) custom-call(s32[8]{0:T(128)S(1)} %copy-done.4, bf16[256,2048]{1,0:T(8,128)(2,1)} %q.11, bf16[256,2048]{1,0:T(8,128)(2,1)} %k.11, bf16[256,2048]{1,0:T(8,128)(2,1)} %v.11, bf16[256,2048]{1,0:T(8,128)(2,1)} %g.11, bf16[8,128,128]{2,1,0:T(8,128)(2,1)S(1)} %pair.2.rest_0_), custom_call_target="tpu_custom_call" | custom-call | bytes 1024 | tf_op jit(solution)/shard_map/states/pallas_call | solution.py:229
  17.3 0.0 copy-start
  17.3 0.1 collective-permute-start.2
  17.4 0.7 %masks.1 = (f32[256,256]{1,0:T(8,128)S(1)}, f32[256,256]{1,0:T(8,128)S(1)}) custom-call(s32[8]{0:T(128)S(1)} %copy-done.4, bf16[8,128,128]{2,1,0:T(8,128)(2,1)S(1)} %pair.2.rest_0_), custom_call_target="tpu_custom_call" | custom-call | bytes 1024 | tf_op jit(solution)/shard_map/masks/pallas_call | solution.py:202
  18.1 0.0 collective-permute-done.3.other
  18.1 0.0 collective-permute-done.4.rest_0_
  18.1 1.3 %collective-permute-done.5.rest_1_ = bf16[8,128,128]{2,1,0:T(8,128)(2,1)S(1)} collective-permute-done((bf16[8,128,128]{2,1,0:T(8,128)(2,1)S(1)}, bf16[8,128,128]{2,1,0:T(8,128)(2,1)S(1)}, u32[]{:S(2)}, u32[]{:S(2)}) %collective-permute-start.5) | collective-permute-done | bytes 262176 | tf_op jit(solution)/shard_map/ppermute | solution.py:215
  19.4 0.7 %join.2 = (f32[4,128,128]{2,1,0:T(8,128)S(1)}, f32[4,128,128]{2,1,0:T(8,128)S(1)}, f32[4,128,128]{2,1,0:T(8,128)S(1)}, f32[4,128,128]{2,1,0:T(8,128)S(1)}) custom-call(s32[8]{0:T(128)S(1)} %copy-done.4, f32[8,128,128]{2,1,0:T(8,128)S(1)} %collective-permute-done.3.other, bf16[8,128,128]{2,1,0:T(8,128)(2,1)S(1)} %collective-permute-done.4.rest_0_, ...), custom_call_target="tpu_custom_call" | custom-call | bytes 1024 | tf_op jit(solution)/shard_map/join/pallas_call | solution.py:202
  20.1 0.1 collective-permute-start.7
  20.2 0.5 collective-permute-start.6
  20.7 0.1 collective-permute-start.1
  20.8 0.9 %collective-permute-done.7.got = f32[4,128,128]{2,1,0:T(8,128)S(1)} collective-permute-done((f32[4,128,128]{2,1,0:T(8,128)S(1)}, f32[4,128,128]{2,1,0:T(8,128)S(1)}, u32[]{:S(2)}, u32[]{:S(2)}) %collective-permute-start.7) | collective-permute-done | bytes 262176 | tf_op jit(solution)/shard_map/ppermute | solution.py:209
  21.7 0.0 copy-done.1
  21.7 0.0 copy-done.2
  21.7 0.0 copy-done.3
  21.7 0.0 copy-done
  21.7 2.2 %grads.4 = (bf16[3,128,512]{2,1,0:T(8,128)(2,1)S(1)}, bf16[3,128,512]{2,1,0:T(8,128)(2,1)S(1)}) custom-call(s32[8]{0:T(128)S(1)} %copy-done.4, bf16[256,2048]{1,0:T(8,128)(2,1)S(1)} %copy-done, bf16[256,2048]{1,0:T(8,128)(2,1)S(1)} %copy-done.1, bf16[256,2048]{1,0:T(8,128)(2,1)S(1)} %copy-done.2, bf16[256,2048]{1,0:T(8,128)(2,1)S(1)} %copy-done.3, ...), custom_call_target="tpu_custom_call" | custom-call | bytes 1024 | tf_op jit(solution)/shard_map/grads/pallas_call | solution.py:202
  23.9 1.6 %collective-permute-start.10 = (bf16[3,128,512]{2,1,0:T(8,128)(2,1)S(1)}, bf16[3,128,512]{2,1,0:T(8,128)(2,1)S(1)}, u32[]{:S(2)}, u32[]{:S(2)}) collective-permute-start(bf16[3,128,512]{2,1,0:T(8,128)(2,1)S(1)} %get-tuple-element.46), channel_id=1, source_target_pairs={{0,1},{1,0},{2,3},{3,2},{4,5},{5,4},{6,7},{7,6},{8,9},{9,8},{10,11... | collective-permute-start | bytes 1179656 | tf_op jit(solution)/shard_map/ppermute | solution.py:221
  25.5 0.0 collective-permute-done.6.got
  25.5 2.1 %grads.5 = (bf16[3,128,512]{2,1,0:T(8,128)(2,1)S(1)}, bf16[3,128,512]{2,1,0:T(8,128)(2,1)S(1)}) custom-call(s32[8]{0:T(128)S(1)} %copy-done.4, bf16[256,2048]{1,0:T(8,128)(2,1)S(1)} %copy-done, bf16[256,2048]{1,0:T(8,128)(2,1)S(1)} %copy-done.1, bf16[256,2048]{1,0:T(8,128)(2,1)S(1)} %copy-done.2, bf16[256,2048]{1,0:T(8,128)(2,1)S(1)} %copy-done.3, ...), custom_call_target="tpu_custom_call" | custom-call | bytes 1024 | tf_op jit(solution)/shard_map/grads/pallas_call | solution.py:202
  27.6 0.0 collective-permute-done.2.got
  27.6 0.6 pair.3
  28.3 2.2 %collective-permute-start.8 = (bf16[8,128,128]{2,1,0:T(8,128)(2,1)S(1)}, bf16[8,128,128]{2,1,0:T(8,128)(2,1)S(1)}, u32[]{:S(2)}, u32[]{:S(2)}) collective-permute-start(bf16[8,128,128]{2,1,0:T(8,128)(2,1)S(1)} %pair.3), channel_id=1, source_target_pairs={{0,6},{4,10},{8,14},{12,18},{16,22},{20,26},{24,30},{6,0},{10,4},{... | collective-permute-start | bytes 786440 | tf_op jit(solution)/shard_map/ppermute | solution.py:215
  30.5 3.6 %collective-permute-start.9 = (bf16[8,128,128]{2,1,0:T(8,128)(2,1)S(1)}, bf16[8,128,128]{2,1,0:T(8,128)(2,1)S(1)}, u32[]{:S(2)}, u32[]{:S(2)}) collective-permute-start(bf16[8,128,128]{2,1,0:T(8,128)(2,1)S(1)} %pair.3), channel_id=1, source_target_pairs={{0,10},{4,14},{8,18},{12,22},{16,26},{20,30},{10,0},{14,4},{18,8},... | collective-permute-start | bytes 786440 | tf_op jit(solution)/shard_map/ppermute | solution.py:215
  34.2 0.6 collective-permute-start.13
  34.8 0.0 collective-permute-done.1.other
  34.8 2.4 %collective-permute-done.8.rest_0_ = bf16[8,128,128]{2,1,0:T(8,128)(2,1)S(1)} collective-permute-done((bf16[8,128,128]{2,1,0:T(8,128)(2,1)S(1)}, bf16[8,128,128]{2,1,0:T(8,128)(2,1)S(1)}, u32[]{:S(2)}, u32[]{:S(2)}) %collective-permute-start.8) | collective-permute-done | bytes 262176 | tf_op jit(solution)/shard_map/ppermute | solution.py:215
  37.2 1.9 %collective-permute-done.9.rest_1_ = bf16[8,128,128]{2,1,0:T(8,128)(2,1)S(1)} collective-permute-done((bf16[8,128,128]{2,1,0:T(8,128)(2,1)S(1)}, bf16[8,128,128]{2,1,0:T(8,128)(2,1)S(1)}, u32[]{:S(2)}, u32[]{:S(2)}) %collective-permute-start.9) | collective-permute-done | bytes 262176 | tf_op jit(solution)/shard_map/ppermute | solution.py:215
  39.1 0.0 collective-permute-done.10.rest_2_.refs_1_
  39.1 0.7 %join.3 = (f32[4,128,128]{2,1,0:T(8,128)S(1)}, f32[4,128,128]{2,1,0:T(8,128)S(1)}, f32[4,128,128]{2,1,0:T(8,128)S(1)}, f32[4,128,128]{2,1,0:T(8,128)S(1)}) custom-call(s32[8]{0:T(128)S(1)} %copy-done.4, f32[8,128,128]{2,1,0:T(8,128)S(1)} %collective-permute-done.1.other, bf16[8,128,128]{2,1,0:T(8,128)(2,1)S(1)} %collective-permute-done.8.rest_0_, ...), custom_call_target="tpu_custom_call" | custom-call | bytes 1024 | tf_op jit(solution)/shard_map/join/pallas_call | solution.py:202
  39.9 0.1 collective-permute-start.12
  39.9 0.5 collective-permute-start.11
  40.4 1.0 %collective-permute-done.12.got = f32[4,128,128]{2,1,0:T(8,128)S(1)} collective-permute-done((f32[4,128,128]{2,1,0:T(8,128)S(1)}, f32[4,128,128]{2,1,0:T(8,128)S(1)}, u32[]{:S(2)}, u32[]{:S(2)}) %collective-permute-start.12) | collective-permute-done | bytes 262176 | tf_op jit(solution)/shard_map/ppermute | solution.py:209
  41.5 2.2 %grads.6 = (bf16[3,128,512]{2,1,0:T(8,128)(2,1)S(1)}, bf16[3,128,512]{2,1,0:T(8,128)(2,1)S(1)}) custom-call(s32[8]{0:T(128)S(1)} %copy-done.4, bf16[256,2048]{1,0:T(8,128)(2,1)S(1)} %copy-done, bf16[256,2048]{1,0:T(8,128)(2,1)S(1)} %copy-done.1, bf16[256,2048]{1,0:T(8,128)(2,1)S(1)} %copy-done.2, bf16[256,2048]{1,0:T(8,128)(2,1)S(1)} %copy-done.3, ...), custom_call_target="tpu_custom_call" | custom-call | bytes 1024 | tf_op jit(solution)/shard_map/grads/pallas_call | solution.py:202
  43.6 0.6 collective-permute-start.15
  44.2 0.0 collective-permute-done.13.rest_1_.refs_1_
  44.2 0.0 collective-permute-done.11.got
  44.2 2.2 %grads.7 = (bf16[3,128,512]{2,1,0:T(8,128)(2,1)S(1)}, bf16[3,128,512]{2,1,0:T(8,128)(2,1)S(1)}) custom-call(s32[8]{0:T(128)S(1)} %copy-done.4, bf16[256,2048]{1,0:T(8,128)(2,1)S(1)} %copy-done, bf16[256,2048]{1,0:T(8,128)(2,1)S(1)} %copy-done.1, bf16[256,2048]{1,0:T(8,128)(2,1)S(1)} %copy-done.2, bf16[256,2048]{1,0:T(8,128)(2,1)S(1)} %copy-done.3, ...), custom_call_target="tpu_custom_call" | custom-call | bytes 1024 | tf_op jit(solution)/shard_map/grads/pallas_call | solution.py:202
  46.4 1.6 %collective-permute-start.14 = (bf16[3,128,512]{2,1,0:T(8,128)(2,1)S(1)}, bf16[3,128,512]{2,1,0:T(8,128)(2,1)S(1)}, u32[]{:S(2)}, u32[]{:S(2)}) collective-permute-start(bf16[3,128,512]{2,1,0:T(8,128)(2,1)S(1)} %get-tuple-element.54), channel_id=1, source_target_pairs={{0,1},{1,0},{2,3},{3,2},{4,5},{5,4},{6,7},{7,6},{8,9},{9,8},{10,11... | collective-permute-start | bytes 1179656 | tf_op jit(solution)/shard_map/ppermute | solution.py:221
  48.0 0.9 %place.4 = (bf16[128,4096]{1,0:T(8,128)(2,1)}, bf16[128,4096]{1,0:T(8,128)(2,1)}, bf16[128,4096]{1,0:T(8,128)(2,1)}) custom-call(bf16[3,128,512]{2,1,0:T(8,128)(2,1)S(1)} %get-tuple-element.44.rest_0_.refs_0_, bf16[3,128,512]{2,1,0:T(8,128)(2,1)S(1)} %collective-permute-done.10.rest_2_.refs_1_), custom_call_target="tpu_custom_call" | custom-call | bytes 1024 | tf_op jit(solution)/shard_map/place/pallas_call | solution.py:273
  48.9 0.9 %place.5 = (bf16[128,4096]{1,0:T(8,128)(2,1)}, bf16[128,4096]{1,0:T(8,128)(2,1)}, bf16[128,4096]{1,0:T(8,128)(2,1)}) custom-call(bf16[3,128,512]{2,1,0:T(8,128)(2,1)S(1)} %get-tuple-element.45.rest_0_.refs_0_, bf16[3,128,512]{2,1,0:T(8,128)(2,1)S(1)} %collective-permute-done.13.rest_1_.refs_1_, ...), custom_call_target="tpu_custom_call", output_to_operand_aliasing={{0}: (2, {}), {1}: (3, {}), {2}: (4, {})} | custom-call | bytes 1024 | tf_op jit(solution)/shard_map/place/pallas_call | solution.py:273
  49.8 5.8 %collective-permute-done.15.refs_1_ = bf16[3,128,512]{2,1,0:T(8,128)(2,1)S(1)} collective-permute-done((bf16[3,128,512]{2,1,0:T(8,128)(2,1)S(1)}, bf16[3,128,512]{2,1,0:T(8,128)(2,1)S(1)}, u32[]{:S(2)}, u32[]{:S(2)}) %collective-permute-start.15) | collective-permute-done | bytes 393248 | tf_op jit(solution)/shard_map/ppermute | solution.py:221
  55.7 0.9 %place.6 = (bf16[128,4096]{1,0:T(8,128)(2,1)}, bf16[128,4096]{1,0:T(8,128)(2,1)}, bf16[128,4096]{1,0:T(8,128)(2,1)}) custom-call(bf16[3,128,512]{2,1,0:T(8,128)(2,1)S(1)} %get-tuple-element.51.rest_0_.refs_0_, bf16[3,128,512]{2,1,0:T(8,128)(2,1)S(1)} %collective-permute-done.15.refs_1_, ...), custom_call_target="tpu_custom_call", output_to_operand_aliasing={{0}: (2, {}), {1}: (3, {}), {2}: (4, {})} | custom-call | bytes 1024 | tf_op jit(solution)/shard_map/place/pallas_call | solution.py:273
  56.6 6.7 %collective-permute-done.14.refs_1_ = bf16[3,128,512]{2,1,0:T(8,128)(2,1)S(1)} collective-permute-done((bf16[3,128,512]{2,1,0:T(8,128)(2,1)S(1)}, bf16[3,128,512]{2,1,0:T(8,128)(2,1)S(1)}, u32[]{:S(2)}, u32[]{:S(2)}) %collective-permute-start.14) | collective-permute-done | bytes 393248 | tf_op jit(solution)/shard_map/ppermute | solution.py:221
  63.3 0.9 %place.7 = (bf16[128,4096]{1,0:T(8,128)(2,1)}, bf16[128,4096]{1,0:T(8,128)(2,1)}, bf16[128,4096]{1,0:T(8,128)(2,1)}) custom-call(bf16[3,128,512]{2,1,0:T(8,128)(2,1)S(1)} %get-tuple-element.53.refs_0_, bf16[3,128,512]{2,1,0:T(8,128)(2,1)S(1)} %collective-permute-done.14.refs_1_, ...), custom_call_target="tpu_custom_call", output_to_operand_aliasing={{0}: (2, {}), {1}: (3, {}), {2}: (4, {})} | custom-call | bytes 1024 | tf_op jit(solution)/shard_map/place/pallas_call | solution.py:273
Async XLA Ops:
  0.6 0.7 %copy-start.4 = (s32[8]{0:T(128)S(1)}, s32[8]{0:T(128)}, u32[]{:S(2)}) copy-start(s32[8]{0:T(128)} %lengths.21) | copy-start | bytes 100
  3.9 2.1 %collective-permute-start = (f32[8,128,128]{2,1,0:T(8,128)S(1)}, f32[8,128,128]{2,1,0:T(8,128)S(1)}, u32[]{:S(2)}, u32[]{:S(2)}) collective-permute-start(f32[8,128,128]{2,1,0:T(8,128)S(1)} %get-tuple-element.35), channel_id=1, source_target_pairs={{0,2},{2,0},{4,6},{6,4},{8,10},{10,8},{12,14},{14,12},{16,18},{18,... | collective-permute-start | bytes 1572872 | tf_op jit(solution)/shard_map/ppermute | solution.py:209
  4.4 13.7 %collective-permute-start.3 = (f32[8,128,128]{2,1,0:T(8,128)S(1)}, f32[8,128,128]{2,1,0:T(8,128)S(1)}, u32[]{:S(2)}, u32[]{:S(2)}) collective-permute-start(f32[8,128,128]{2,1,0:T(8,128)S(1)} %get-tuple-element.34.kept), channel_id=1, source_target_pairs={{0,2},{2,0},{4,6},{6,4},{8,10},{10,8},{12,14},{14,12},{16,18},{18,... | collective-permute-start | bytes 1572872 | tf_op jit(solution)/shard_map/ppermute | solution.py:209
  6.5 11.6 %collective-permute-start.4 = (bf16[8,128,128]{2,1,0:T(8,128)(2,1)S(1)}, bf16[8,128,128]{2,1,0:T(8,128)(2,1)S(1)}, u32[]{:S(2)}, u32[]{:S(2)}) collective-permute-start(bf16[8,128,128]{2,1,0:T(8,128)(2,1)S(1)} %pair.2.rest_0_), channel_id=1, source_target_pairs={{0,6},{4,10},{8,14},{12,18},{16,22},{20,26},{24,30},{6,0},{10,4},{... | collective-permute-start | bytes 786440 | tf_op jit(solution)/shard_map/ppermute | solution.py:215
  11.1 8.3 %collective-permute-start.5 = (bf16[8,128,128]{2,1,0:T(8,128)(2,1)S(1)}, bf16[8,128,128]{2,1,0:T(8,128)(2,1)S(1)}, u32[]{:S(2)}, u32[]{:S(2)}) collective-permute-start(bf16[8,128,128]{2,1,0:T(8,128)(2,1)S(1)} %pair.2.rest_0_), channel_id=1, source_target_pairs={{0,10},{4,14},{8,18},{12,22},{16,26},{20,30},{10,0},{14,4},{18,8},... | collective-permute-start | bytes 786440 | tf_op jit(solution)/shard_map/ppermute | solution.py:215
  14.4 7.3 %copy-start.1 = (bf16[256,2048]{1,0:T(8,128)(2,1)S(1)}, bf16[256,2048]{1,0:T(8,128)(2,1)}, u32[]{:S(2)}) copy-start(bf16[256,2048]{1,0:T(8,128)(2,1)} %k.11) | copy-start | bytes 3145732
  14.4 7.3 %copy-start.2 = (bf16[256,2048]{1,0:T(8,128)(2,1)S(1)}, bf16[256,2048]{1,0:T(8,128)(2,1)}, u32[]{:S(2)}) copy-start(bf16[256,2048]{1,0:T(8,128)(2,1)} %v.11) | copy-start | bytes 3145732
  14.5 7.3 %copy-start.3 = (bf16[256,2048]{1,0:T(8,128)(2,1)S(1)}, bf16[256,2048]{1,0:T(8,128)(2,1)}, u32[]{:S(2)}) copy-start(bf16[256,2048]{1,0:T(8,128)(2,1)} %g.11) | copy-start | bytes 3145732
  17.3 4.4 %copy-start = (bf16[256,2048]{1,0:T(8,128)(2,1)S(1)}, bf16[256,2048]{1,0:T(8,128)(2,1)}, u32[]{:S(2)}) copy-start(bf16[256,2048]{1,0:T(8,128)(2,1)} %q.11) | copy-start | bytes 3145732
  17.3 10.3 %collective-permute-start.2 = (f32[8,128,128]{2,1,0:T(8,128)S(1)}, f32[8,128,128]{2,1,0:T(8,128)S(1)}, u32[]{:S(2)}, u32[]{:S(2)}) collective-permute-start(f32[8,128,128]{2,1,0:T(8,128)S(1)} %get-tuple-element.39), channel_id=1, source_target_pairs={{0,2},{2,0},{4,6},{6,4},{8,10},{10,8},{12,14},{14,12},{16,18},{18,... | collective-permute-start | bytes 1572872 | tf_op jit(solution)/shard_map/ppermute | solution.py:209
  20.1 1.6 %collective-permute-start.7 = (f32[4,128,128]{2,1,0:T(8,128)S(1)}, f32[4,128,128]{2,1,0:T(8,128)S(1)}, u32[]{:S(2)}, u32[]{:S(2)}) collective-permute-start(f32[4,128,128]{2,1,0:T(8,128)S(1)} %get-tuple-element.43), channel_id=1, source_target_pairs={{0,2},{2,0},{4,6},{6,4},{8,10},{10,8},{12,14},{14,12},{16,18},{18,... | collective-permute-start | bytes 786440 | tf_op jit(solution)/shard_map/ppermute | solution.py:209
  20.2 5.3 %collective-permute-start.6 = (f32[4,128,128]{2,1,0:T(8,128)S(1)}, f32[4,128,128]{2,1,0:T(8,128)S(1)}, u32[]{:S(2)}, u32[]{:S(2)}) collective-permute-start(f32[4,128,128]{2,1,0:T(8,128)S(1)} %get-tuple-element.41), channel_id=1, source_target_pairs={{0,2},{2,0},{4,6},{6,4},{8,10},{10,8},{12,14},{14,12},{16,18},{18,... | collective-permute-start | bytes 786440 | tf_op jit(solution)/shard_map/ppermute | solution.py:209
  20.7 14.1 %collective-permute-start.1 = (f32[8,128,128]{2,1,0:T(8,128)S(1)}, f32[8,128,128]{2,1,0:T(8,128)S(1)}, u32[]{:S(2)}, u32[]{:S(2)}) collective-permute-start(f32[8,128,128]{2,1,0:T(8,128)S(1)} %get-tuple-element.38.kept), channel_id=1, source_target_pairs={{0,2},{2,0},{4,6},{6,4},{8,10},{10,8},{12,14},{14,12},{16,18},{18,... | collective-permute-start | bytes 1572872 | tf_op jit(solution)/shard_map/ppermute | solution.py:209
  23.9 15.2 %collective-permute-start.10 = (bf16[3,128,512]{2,1,0:T(8,128)(2,1)S(1)}, bf16[3,128,512]{2,1,0:T(8,128)(2,1)S(1)}, u32[]{:S(2)}, u32[]{:S(2)}) collective-permute-start(bf16[3,128,512]{2,1,0:T(8,128)(2,1)S(1)} %get-tuple-element.46), channel_id=1, source_target_pairs={{0,1},{1,0},{2,3},{3,2},{4,5},{5,4},{6,7},{7,6},{8,9},{9,8},{10,11... | collective-permute-start | bytes 1179656 | tf_op jit(solution)/shard_map/ppermute | solution.py:221
  28.3 8.9 %collective-permute-start.8 = (bf16[8,128,128]{2,1,0:T(8,128)(2,1)S(1)}, bf16[8,128,128]{2,1,0:T(8,128)(2,1)S(1)}, u32[]{:S(2)}, u32[]{:S(2)}) collective-permute-start(bf16[8,128,128]{2,1,0:T(8,128)(2,1)S(1)} %pair.3), channel_id=1, source_target_pairs={{0,6},{4,10},{8,14},{12,18},{16,22},{20,26},{24,30},{6,0},{10,4},{... | collective-permute-start | bytes 786440 | tf_op jit(solution)/shard_map/ppermute | solution.py:215
  30.5 8.6 %collective-permute-start.9 = (bf16[8,128,128]{2,1,0:T(8,128)(2,1)S(1)}, bf16[8,128,128]{2,1,0:T(8,128)(2,1)S(1)}, u32[]{:S(2)}, u32[]{:S(2)}) collective-permute-start(bf16[8,128,128]{2,1,0:T(8,128)(2,1)S(1)} %pair.3), channel_id=1, source_target_pairs={{0,10},{4,14},{8,18},{12,22},{16,26},{20,30},{10,0},{14,4},{18,8},... | collective-permute-start | bytes 786440 | tf_op jit(solution)/shard_map/ppermute | solution.py:215
  34.2 10.1 %collective-permute-start.13 = (bf16[3,128,512]{2,1,0:T(8,128)(2,1)S(1)}, bf16[3,128,512]{2,1,0:T(8,128)(2,1)S(1)}, u32[]{:S(2)}, u32[]{:S(2)}) collective-permute-start(bf16[3,128,512]{2,1,0:T(8,128)(2,1)S(1)} %get-tuple-element.52), channel_id=1, source_target_pairs={{0,1},{1,0},{2,3},{3,2},{4,5},{5,4},{6,7},{7,6},{8,9},{9,8},{10,11... | collective-permute-start | bytes 1179656 | tf_op jit(solution)/shard_map/ppermute | solution.py:221
  39.9 1.6 %collective-permute-start.12 = (f32[4,128,128]{2,1,0:T(8,128)S(1)}, f32[4,128,128]{2,1,0:T(8,128)S(1)}, u32[]{:S(2)}, u32[]{:S(2)}) collective-permute-start(f32[4,128,128]{2,1,0:T(8,128)S(1)} %get-tuple-element.50), channel_id=1, source_target_pairs={{0,2},{2,0},{4,6},{6,4},{8,10},{10,8},{12,14},{14,12},{16,18},{18,... | collective-permute-start | bytes 786440 | tf_op jit(solution)/shard_map/ppermute | solution.py:209
  39.9 4.3 %collective-permute-start.11 = (f32[4,128,128]{2,1,0:T(8,128)S(1)}, f32[4,128,128]{2,1,0:T(8,128)S(1)}, u32[]{:S(2)}, u32[]{:S(2)}) collective-permute-start(f32[4,128,128]{2,1,0:T(8,128)S(1)} %get-tuple-element.48), channel_id=1, source_target_pairs={{0,2},{2,0},{4,6},{6,4},{8,10},{10,8},{12,14},{14,12},{16,18},{18,... | collective-permute-start | bytes 786440 | tf_op jit(solution)/shard_map/ppermute | solution.py:209
  43.6 12.0 %collective-permute-start.15 = (bf16[3,128,512]{2,1,0:T(8,128)(2,1)S(1)}, bf16[3,128,512]{2,1,0:T(8,128)(2,1)S(1)}, u32[]{:S(2)}, u32[]{:S(2)}) collective-permute-start(bf16[3,128,512]{2,1,0:T(8,128)(2,1)S(1)} %get-tuple-element.55), channel_id=1, source_target_pairs={{0,1},{1,0},{2,3},{3,2},{4,5},{5,4},{6,7},{7,6},{8,9},{9,8},{10,11... | collective-permute-start | bytes 1179656 | tf_op jit(solution)/shard_map/ppermute | solution.py:221
  46.4 16.9 %collective-permute-start.14 = (bf16[3,128,512]{2,1,0:T(8,128)(2,1)S(1)}, bf16[3,128,512]{2,1,0:T(8,128)(2,1)S(1)}, u32[]{:S(2)}, u32[]{:S(2)}) collective-permute-start(bf16[3,128,512]{2,1,0:T(8,128)(2,1)S(1)} %get-tuple-element.54), channel_id=1, source_target_pairs={{0,1},{1,0},{2,3},{3,2},{4,5},{5,4},{6,7},{7,6},{8,9},{9,8},{10,11... | collective-permute-start | bytes 1179656 | tf_op jit(solution)/shard_map/ppermute | solution.py:221

commit v3 on v2

--- a/solution.py
+++ b/solution.py
@@ -9,7 +9,7 @@
 
 HEAD_DIM = 128
 MOST = 1024
-GROUP = 4
+GROUP = 2
 CHUNK = 4
 LINK = jnp.bfloat16
 VMEM_LIMIT = 16 * 1024 * 1024
@@ -42,7 +42,7 @@
 
 
 def state_kernel(lengths, q, k, v, g, *rest, ndocs, rows, offset, heads, group):
-    kept, sent, held, sems = rest[-4:]
+    kept, sent, handed, held, sems = rest[-5:]
     gw = group * HEAD_DIM
     copies = []
     for c in range(heads // group):
@@ -50,6 +50,8 @@
             src = ref.at[:, pl.ds(offset + c * gw, gw)]
             copies.append(pltpu.make_async_copy(src, held.at[i, :, pl.ds(c * gw, gw)], sems.at[c, i]))
             copies[-1].start()
+    for i in range(ndocs):
+        handed[i] = lengths[i]
     place = lax.axis_index("seq")
     first_core = lax.rem(place, 2) == 0
     _, _, _, _, first, last = block_range(lengths, ndocs, place * rows, rows)
@@ -199,20 +201,21 @@
         return jax.ShapeDtypeStruct(dims, dtype)
 
     def call(name, kernel, args, outs, scratch=(), after=(), limit=VMEM_LIMIT):
+        lengths, *args = args
         return pl.pallas_call(
             kernel, in_specs=[in_smem] + [in_vmem] * len(args) + [anywhere] * len(after), out_specs=[in_vmem] * len(outs), out_shape=outs,
             scratch_shapes=list(scratch), cost_estimate=cheap,
             compiler_params=pltpu.CompilerParams(vmem_limit_bytes=limit), name=name,
-        )(doc_lengths, *args, *after)
+        )(lengths, *args, *after)
 
     def swap_cores(a):
         return lax.ppermute(a, "seq", [(b, b ^ 1) for b in range(seq)])
 
     def swap_pairs(sent):
         came = []
-        for hop in range(1, hops + 1):
+        for hop in range(hops, 0, -1):
             perm = [(2 * m, 2 * (m + hop) + 1) for m in range(pairs - hop)]
-            came.append(lax.ppermute(sent, "seq", perm + [(b, a) for a, b in perm]))
+            came.insert(0, lax.ppermute(sent, "seq", perm + [(b, a) for a, b in perm]))
         return came
 
     def send_rows(outs):
@@ -223,48 +226,47 @@
 
     square = (HEAD_DIM, HEAD_DIM)
 
-    def states(offset, half, after):
+    def states(lengths, offset, half, after):
         heads = half // HEAD_DIM
         group = GROUP if heads % GROUP == 0 else 2
-        kept, sent = pl.pallas_call(
+        return pl.pallas_call(
             functools.partial(state_kernel, offset=offset, heads=heads, group=group, **sizes),
-            in_specs=[in_smem] + [anywhere] * (4 + len(after)), out_specs=[in_vmem] * 2,
-            out_shape=[shape_of(heads, *square)] * 2,
+            in_specs=[in_smem] + [anywhere] * (4 + len(after)), out_specs=[in_vmem] * 2 + [in_smem],
+            out_shape=[shape_of(heads, *square)] * 2 + [shape_of(ndocs, dtype=jnp.int32)],
             scratch_shapes=[pltpu.VMEM((4, rows, half), bf16), pltpu.SemaphoreType.DMA((heads // group, 4))],
             cost_estimate=cheap, compiler_params=pltpu.CompilerParams(vmem_limit_bytes=FIRST_LIMIT), name="states",
-        )(doc_lengths, *inputs, *after)
-        return kept, sent
-
-    def pair_up(kept, got, after):
+        )(lengths, *inputs, *after)
+
+    def pair_up(lengths, kept, got, after):
         out = shape_of(*kept.shape, dtype=LINK)
-        total = call("pair", functools.partial(pair_kernel, **sizes), (kept, got), [out], after=after)[0]
+        total = call("pair", functools.partial(pair_kernel, **sizes), (lengths, kept, got), [out], after=after)[0]
         return total, swap_pairs(total)
 
-    def join(kept, came, chunks, after):
+    def join(lengths, kept, came, chunks, after):
         counts = [cw // HEAD_DIM for _, cw in chunks]
         joined = call(
-            "join", functools.partial(join_kernel, counts=counts, hops=hops, **sizes), (swap_cores(kept), *came),
+            "join", functools.partial(join_kernel, counts=counts, hops=hops, **sizes), (lengths, swap_cores(kept), *came),
             [shape_of(n, *square) for n in counts] * 2, after=after,
         )
         return [(mine, swap_cores(theirs)) for mine, theirs in zip(joined[:len(chunks)], joined[len(chunks):])]
 
-    def grads(masks, offset, cw, mine, theirs, after):
+    def grads(lengths, masks, offset, cw, mine, theirs, after):
         return call(
             "grads", functools.partial(grad_kernel, offset=offset, heads=cw // HEAD_DIM, groups=groups, **sizes),
-            (*inputs, *masks, mine, theirs), [shape_of(3, part, cw, dtype=bf16)] * groups,
+            (lengths, *inputs, *masks, mine, theirs), [shape_of(3, part, cw, dtype=bf16)] * groups,
             [pltpu.VMEM((3, rows, cw), bf16)], after, GRAD_LIMIT,
         )
 
-    cuts, outs, arrived, totals, masks = [], [], [], [], None
+    cuts, outs, arrived, totals, masks, lengths = [], [], [], [], None, doc_lengths
     for start, half, chunks in halves:
-        kept, sent = states(start, half, totals)
-        total, came = pair_up(kept, swap_cores(sent), [made[0] for made in outs[-1:]])
+        kept, sent, lengths = states(lengths, start, half, totals)
+        total, came = pair_up(lengths, kept, swap_cores(sent), [made[0] for made in outs[:1]])
         totals = [total]
-        masks = masks or call("masks", functools.partial(mask_kernel, **sizes), (), [shape_of(rows, rows)] * 2, after=totals)
-        joined = join(kept, came, chunks, [parts[1] for parts in arrived[:1]] or masks[:1])
+        masks = masks or call("masks", functools.partial(mask_kernel, **sizes), (lengths,), [shape_of(rows, rows)] * 2, after=totals)
+        joined = join(lengths, kept, came, chunks, [parts[1] for parts in arrived[:1]] or masks[:1])
         for (offset, cw), (mine, theirs) in zip(chunks, joined):
             after = [made[0] for made in outs[-1:]] + [parts[1] for parts in arrived[1:-1]][-1:]
-            outs.append(grads(masks, offset, cw, mine, theirs, after))
+            outs.append(grads(lengths, masks, offset, cw, mine, theirs, after))
             arrived.append(send_rows(outs[-1]))
         cuts += chunks
 

time: 64.5 us -> 67 us (1.039)
  Pallas kernels: 21.1 us -> 22.6 us
    pallas_call x2, Pallas kernels: 5.4 us -> 6.88 us  [states(): pl.pallas_call(functools.partial(state_kernel, offset=offset, heads=heads...]
  transfers between devices with their start and end apart: 16 -> 16, of which waited for: 8 -> 7; matrix products, arithmetic and copies ran while one was open for 0% -> 0% of each run, Pallas kernels for 27% -> 28%
where the time goes in v3:
time: 67 us; the launch traced here: 66.3 us
  Pallas kernels  22.6 us (34%)
  waiting for transfers between devices  22.2 us (33%)
  starting transfers between devices  20 us (30%)
  between operations  0.85 us (1%)
  local copies, waits for them, and re-layouts  0.67 us (1%)
    ppermute x4, starting transfers between devices, swap_pairs(): came.insert(0, lax.ppermute(sent, 'seq', perm + [(b, a) for a, b in perm]))  13.9 us
    ppermute x4, waiting for transfers between devices, send_rows(): lax.ppermute(outs[j], 'head', [(x, (x + j) % groups) for x in range(group...  12.5 us
    pallas_call x9, Pallas kernels, call(): pl.pallas_call(kernel, in_specs=[in_smem] + [in_vmem] * len(args) + [anyw...  12 us
    pallas_call x2, Pallas kernels, states(): pl.pallas_call(functools.partial(state_kernel, offset=offset, heads=heads...  6.88 us
    ppermute x4, waiting for transfers between devices, swap_pairs(): came.insert(0, lax.ppermute(sent, 'seq', perm + [(b, a) for a, b in perm]))  6.17 us
    ppermute x4, starting transfers between devices, send_rows(): lax.ppermute(outs[j], 'head', [(x, (x + j) % groups) for x in range(group...  4.32 us
    pallas_call x4, Pallas kernels, shards(): pl.pallas_call(functools.partial(place_kernel, groups=groups, offset=offs...  3.7 us
    ppermute x8, waiting for transfers between devices, swap_cores(): return lax.ppermute(a, 'seq', [(b, b ^ 1) for b in range(seq)])  3.52 us
  transfers between devices with their start and end apart: 16, of which 7 were waited for; matrix products, arithmetic and copies ran while one was open for 0% of the time, Pallas kernels for 28%

profile of v3, /device:TPU:0, one launch (start us, length us, event | category | flops | bytes accessed | tf_op | source)
XLA Modules:
  0.0 66.3 jit_solution(14103951159398116675)
XLA Ops:
  0.6 0.0 copy-start.4
  0.6 0.6 copy-done.4
  1.3 3.3 %states.2 = (f32[8,128,128]{2,1,0:T(8,128)S(1)}, f32[8,128,128]{2,1,0:T(8,128)S(1)}, s32[8]{0:T(128)S(1)}) custom-call(s32[8]{0:T(128)S(1)} %copy-done.4, bf16[256,2048]{1,0:T(8,128)(2,1)} %q.11, bf16[256,2048]{1,0:T(8,128)(2,1)} %k.11, bf16[256,2048]{1,0:T(8,128)(2,1)} %v.11, bf16[256,2048]{1,0:T(8,128)(2,1)} %g.11), custom_call_target="tpu_custom_call" | custom-call | bytes 1024 | tf_op jit(solution)/shard_map/states/pallas_call | solution.py:232
  4.6 0.5 collective-permute-start
  5.1 0.1 collective-permute-start.3
  5.2 1.5 %collective-permute-done.got = f32[8,128,128]{2,1,0:T(8,128)S(1)} collective-permute-done((f32[8,128,128]{2,1,0:T(8,128)S(1)}, f32[8,128,128]{2,1,0:T(8,128)S(1)}, u32[]{:S(2)}, u32[]{:S(2)}) %collective-permute-start) | collective-permute-done | bytes 524320 | tf_op jit(solution)/shard_map/ppermute | solution.py:212
  6.7 0.6 pair.2.rest_0_
  7.3 4.6 %collective-permute-start.5 = (bf16[8,128,128]{2,1,0:T(8,128)(2,1)S(1)}, bf16[8,128,128]{2,1,0:T(8,128)(2,1)S(1)}, u32[]{:S(2)}, u32[]{:S(2)}) collective-permute-start(bf16[8,128,128]{2,1,0:T(8,128)(2,1)S(1)} %pair.2.rest_0_), channel_id=1, source_target_pairs={{0,10},{4,14},{8,18},{12,22},{16,26},{20,30},{10,0},{14,4},{18,8},... | collective-permute-start | bytes 786440 | tf_op jit(solution)/shard_map/ppermute | solution.py:218
  11.9 1.9 %collective-permute-start.4 = (bf16[8,128,128]{2,1,0:T(8,128)(2,1)S(1)}, bf16[8,128,128]{2,1,0:T(8,128)(2,1)S(1)}, u32[]{:S(2)}, u32[]{:S(2)}) collective-permute-start(bf16[8,128,128]{2,1,0:T(8,128)(2,1)S(1)} %pair.2.rest_0_), channel_id=1, source_target_pairs={{0,6},{4,10},{8,14},{12,18},{16,22},{20,26},{24,30},{6,0},{10,4},{... | collective-permute-start | bytes 786440 | tf_op jit(solution)/shard_map/ppermute | solution.py:218
  13.8 0.0 copy-start.1
  13.8 0.0 copy-start.2
  13.8 0.0 copy-start.3
  13.8 3.6 %states.3 = (f32[8,128,128]{2,1,0:T(8,128)S(1)}, f32[8,128,128]{2,1,0:T(8,128)S(1)}, s32[8]{0:T(128)S(1)}) custom-call(s32[8]{0:T(128)S(1)} %get-tuple-element.36.lengths, bf16[256,2048]{1,0:T(8,128)(2,1)} %q.11, bf16[256,2048]{1,0:T(8,128)(2,1)} %k.11, bf16[256,2048]{1,0:T(8,128)(2,1)} %v.11, bf16[256,2048]{1,0:T(8,128)(2,1)} %g.11, ...), custom_call_target="tpu_custom_call" | custom-call | bytes 1024 | tf_op jit(solution)/shard_map/states/pallas_call | solution.py:232
  17.4 0.0 copy-start
  17.4 0.1 collective-permute-start.2
  17.5 0.7 %masks.1 = (f32[256,256]{1,0:T(8,128)S(1)}, f32[256,256]{1,0:T(8,128)S(1)}) custom-call(s32[8]{0:T(128)S(1)} %get-tuple-element.36.lengths, bf16[8,128,128]{2,1,0:T(8,128)(2,1)S(1)} %pair.2.rest_0_), custom_call_target="tpu_custom_call" | custom-call | bytes 1024 | tf_op jit(solution)/shard_map/masks/pallas_call | solution.py:205
  18.2 0.0 collective-permute-done.3.other
  18.2 0.0 collective-permute-done.5.rest_1_
  18.2 2.3 %collective-permute-done.4.rest_0_ = bf16[8,128,128]{2,1,0:T(8,128)(2,1)S(1)} collective-permute-done((bf16[8,128,128]{2,1,0:T(8,128)(2,1)S(1)}, bf16[8,128,128]{2,1,0:T(8,128)(2,1)S(1)}, u32[]{:S(2)}, u32[]{:S(2)}) %collective-permute-start.4) | collective-permute-done | bytes 262176 | tf_op jit(solution)/shard_map/ppermute | solution.py:218
  20.5 0.7 %join.2 = (f32[4,128,128]{2,1,0:T(8,128)S(1)}, f32[4,128,128]{2,1,0:T(8,128)S(1)}, f32[4,128,128]{2,1,0:T(8,128)S(1)}, f32[4,128,128]{2,1,0:T(8,128)S(1)}) custom-call(s32[8]{0:T(128)S(1)} %get-tuple-element.36.lengths, f32[8,128,128]{2,1,0:T(8,128)S(1)} %collective-permute-done.3.other, bf16[8,128,128]{2,1,0:T(8,128)(2,1)S(1)} %collective-permute-done.4.rest_0_, ...), custom_call_target="tpu_custom_call" | custom-call | bytes 1024 | tf_op jit(solution)/shard_map/join/pallas_call | solution.py:205
  21.2 0.1 collective-permute-start.6
  21.3 0.5 collective-permute-start.1
  21.8 1.0 %collective-permute-done.6.got = f32[4,128,128]{2,1,0:T(8,128)S(1)} collective-permute-done((f32[4,128,128]{2,1,0:T(8,128)S(1)}, f32[4,128,128]{2,1,0:T(8,128)S(1)}, u32[]{:S(2)}, u32[]{:S(2)}) %collective-permute-start.6) | collective-permute-done | bytes 262176 | tf_op jit(solution)/shard_map/ppermute | solution.py:212
  22.8 0.0 copy-done.1
  22.8 0.0 copy-done.2
  22.8 0.0 copy-done.3
  22.8 0.0 copy-done
  22.8 2.2 %grads.4 = (bf16[3,128,512]{2,1,0:T(8,128)(2,1)S(1)}, bf16[3,128,512]{2,1,0:T(8,128)(2,1)S(1)}) custom-call(s32[8]{0:T(128)S(1)} %get-tuple-element.36.lengths, bf16[256,2048]{1,0:T(8,128)(2,1)S(1)} %copy-done, bf16[256,2048]{1,0:T(8,128)(2,1)S(1)} %copy-done.1, bf16[256,2048]{1,0:T(8,128)(2,1)S(1)} %copy-done.2, bf16[256,2048]{1,0:T(8,128)(2,1)S(1)} %copy-done.3, ...), custom_call_target="tpu_custom_call" | custom-call | bytes 1024 | tf_op jit(solution)/shard_map/grads/pallas_call | solution.py:205
  25.0 1.6 %collective-permute-start.9 = (bf16[3,128,512]{2,1,0:T(8,128)(2,1)S(1)}, bf16[3,128,512]{2,1,0:T(8,128)(2,1)S(1)}, u32[]{:S(2)}, u32[]{:S(2)}) collective-permute-start(bf16[3,128,512]{2,1,0:T(8,128)(2,1)S(1)} %get-tuple-element.47), channel_id=1, source_target_pairs={{0,1},{1,0},{2,3},{3,2},{4,5},{5,4},{6,7},{7,6},{8,9},{9,8},{10,11... | collective-permute-start | bytes 1179656 | tf_op jit(solution)/shard_map/ppermute | solution.py:224
  26.6 0.0 collective-permute-start.12
  26.6 0.0 collective-permute-done.2.got
  26.6 0.6 pair.3
  27.2 5.5 %collective-permute-start.8 = (bf16[8,128,128]{2,1,0:T(8,128)(2,1)S(1)}, bf16[8,128,128]{2,1,0:T(8,128)(2,1)S(1)}, u32[]{:S(2)}, u32[]{:S(2)}) collective-permute-start(bf16[8,128,128]{2,1,0:T(8,128)(2,1)S(1)} %pair.3), channel_id=1, source_target_pairs={{0,10},{4,14},{8,18},{12,22},{16,26},{20,30},{10,0},{14,4},{18,8},... | collective-permute-start | bytes 786440 | tf_op jit(solution)/shard_map/ppermute | solution.py:218
  32.7 1.9 %collective-permute-start.7 = (bf16[8,128,128]{2,1,0:T(8,128)(2,1)S(1)}, bf16[8,128,128]{2,1,0:T(8,128)(2,1)S(1)}, u32[]{:S(2)}, u32[]{:S(2)}) collective-permute-start(bf16[8,128,128]{2,1,0:T(8,128)(2,1)S(1)} %pair.3), channel_id=1, source_target_pairs={{0,6},{4,10},{8,14},{12,18},{16,22},{20,26},{24,30},{6,0},{10,4},{... | collective-permute-start | bytes 786440 | tf_op jit(solution)/shard_map/ppermute | solution.py:218
  34.6 0.0 collective-permute-done.12.got
  34.6 2.2 %grads.5 = (bf16[3,128,512]{2,1,0:T(8,128)(2,1)S(1)}, bf16[3,128,512]{2,1,0:T(8,128)(2,1)S(1)}) custom-call(s32[8]{0:T(128)S(1)} %get-tuple-element.36.lengths, bf16[256,2048]{1,0:T(8,128)(2,1)S(1)} %copy-done, bf16[256,2048]{1,0:T(8,128)(2,1)S(1)} %copy-done.1, bf16[256,2048]{1,0:T(8,128)(2,1)S(1)} %copy-done.2, bf16[256,2048]{1,0:T(8,128)(2,1)S(1)} %copy-done.3, ...), custom_call_target="tpu_custom_call" | custom-call | bytes 1024 | tf_op jit(solution)/shard_map/grads/pallas_call | solution.py:205
  36.8 0.6 collective-permute-start.13
  37.4 0.0 collective-permute-done.1.other
  37.4 0.0 collective-permute-done.8.rest_1_
  37.4 3.9 %collective-permute-done.7.rest_0_ = bf16[8,128,128]{2,1,0:T(8,128)(2,1)S(1)} collective-permute-done((bf16[8,128,128]{2,1,0:T(8,128)(2,1)S(1)}, bf16[8,128,128]{2,1,0:T(8,128)(2,1)S(1)}, u32[]{:S(2)}, u32[]{:S(2)}) %collective-permute-start.7) | collective-permute-done | bytes 262176 | tf_op jit(solution)/shard_map/ppermute | solution.py:218
  41.3 0.0 collective-permute-done.9.rest_2_.refs_1_
  41.3 0.7 %join.3 = (f32[4,128,128]{2,1,0:T(8,128)S(1)}, f32[4,128,128]{2,1,0:T(8,128)S(1)}, f32[4,128,128]{2,1,0:T(8,128)S(1)}, f32[4,128,128]{2,1,0:T(8,128)S(1)}) custom-call(s32[8]{0:T(128)S(1)} %get-tuple-element.39.lengths, f32[8,128,128]{2,1,0:T(8,128)S(1)} %collective-permute-done.1.other, bf16[8,128,128]{2,1,0:T(8,128)(2,1)S(1)} %collective-permute-done.7.rest_0_, ...), custom_call_target="tpu_custom_call" | custom-call | bytes 1024 | tf_op jit(solution)/shard_map/join/pallas_call | solution.py:205
  42.0 0.1 collective-permute-start.11
  42.1 0.5 collective-permute-start.10
  42.6 1.0 %collective-permute-done.11.got = f32[4,128,128]{2,1,0:T(8,128)S(1)} collective-permute-done((f32[4,128,128]{2,1,0:T(8,128)S(1)}, f32[4,128,128]{2,1,0:T(8,128)S(1)}, u32[]{:S(2)}, u32[]{:S(2)}) %collective-permute-start.11) | collective-permute-done | bytes 262176 | tf_op jit(solution)/shard_map/ppermute | solution.py:212
  43.6 2.2 %grads.6 = (bf16[3,128,512]{2,1,0:T(8,128)(2,1)S(1)}, bf16[3,128,512]{2,1,0:T(8,128)(2,1)S(1)}) custom-call(s32[8]{0:T(128)S(1)} %get-tuple-element.39.lengths, bf16[256,2048]{1,0:T(8,128)(2,1)S(1)} %copy-done, bf16[256,2048]{1,0:T(8,128)(2,1)S(1)} %copy-done.1, bf16[256,2048]{1,0:T(8,128)(2,1)S(1)} %copy-done.2, bf16[256,2048]{1,0:T(8,128)(2,1)S(1)} %copy-done.3, ...), custom_call_target="tpu_custom_call" | custom-call | bytes 1024 | tf_op jit(solution)/shard_map/grads/pallas_call | solution.py:205
  45.8 0.6 collective-permute-start.15
  46.4 0.0 collective-permute-done.13.rest_1_.refs_1_
  46.4 0.0 collective-permute-done.10.got
  46.4 2.2 %grads.7 = (bf16[3,128,512]{2,1,0:T(8,128)(2,1)S(1)}, bf16[3,128,512]{2,1,0:T(8,128)(2,1)S(1)}) custom-call(s32[8]{0:T(128)S(1)} %get-tuple-element.39.lengths, bf16[256,2048]{1,0:T(8,128)(2,1)S(1)} %copy-done, bf16[256,2048]{1,0:T(8,128)(2,1)S(1)} %copy-done.1, bf16[256,2048]{1,0:T(8,128)(2,1)S(1)} %copy-done.2, bf16[256,2048]{1,0:T(8,128)(2,1)S(1)} %copy-done.3, ...), custom_call_target="tpu_custom_call" | custom-call | bytes 1024 | tf_op jit(solution)/shard_map/grads/pallas_call | solution.py:205
  48.5 1.6 %collective-permute-start.14 = (bf16[3,128,512]{2,1,0:T(8,128)(2,1)S(1)}, bf16[3,128,512]{2,1,0:T(8,128)(2,1)S(1)}, u32[]{:S(2)}, u32[]{:S(2)}) collective-permute-start(bf16[3,128,512]{2,1,0:T(8,128)(2,1)S(1)} %get-tuple-element.58), channel_id=1, source_target_pairs={{0,1},{1,0},{2,3},{3,2},{4,5},{5,4},{6,7},{7,6},{8,9},{9,8},{10,11... | collective-permute-start | bytes 1179656 | tf_op jit(solution)/shard_map/ppermute | solution.py:224
  50.1 0.9 %place.4 = (bf16[128,4096]{1,0:T(8,128)(2,1)}, bf16[128,4096]{1,0:T(8,128)(2,1)}, bf16[128,4096]{1,0:T(8,128)(2,1)}) custom-call(bf16[3,128,512]{2,1,0:T(8,128)(2,1)S(1)} %get-tuple-element.46.rest_0_.refs_0_, bf16[3,128,512]{2,1,0:T(8,128)(2,1)S(1)} %collective-permute-done.9.rest_2_.refs_1_), custom_call_target="tpu_custom_call" | custom-call | bytes 1024 | tf_op jit(solution)/shard_map/place/pallas_call | solution.py:275
  51.0 0.9 %place.5 = (bf16[128,4096]{1,0:T(8,128)(2,1)}, bf16[128,4096]{1,0:T(8,128)(2,1)}, bf16[128,4096]{1,0:T(8,128)(2,1)}) custom-call(bf16[3,128,512]{2,1,0:T(8,128)(2,1)S(1)} %get-tuple-element.54.rest_0_.refs_0_, bf16[3,128,512]{2,1,0:T(8,128)(2,1)S(1)} %collective-permute-done.13.rest_1_.refs_1_, ...), custom_call_target="tpu_custom_call", output_to_operand_aliasing={{0}: (2, {}), {1}: (3, {}), {2}: (4, {})} | custom-call | bytes 1024 | tf_op jit(solution)/shard_map/place/pallas_call | solution.py:275
  52.0 5.8 %collective-permute-done.15.refs_1_ = bf16[3,128,512]{2,1,0:T(8,128)(2,1)S(1)} collective-permute-done((bf16[3,128,512]{2,1,0:T(8,128)(2,1)S(1)}, bf16[3,128,512]{2,1,0:T(8,128)(2,1)S(1)}, u32[]{:S(2)}, u32[]{:S(2)}) %collective-permute-start.15) | collective-permute-done | bytes 393248 | tf_op jit(solution)/shard_map/ppermute | solution.py:224
  57.8 0.9 %place.6 = (bf16[128,4096]{1,0:T(8,128)(2,1)}, bf16[128,4096]{1,0:T(8,128)(2,1)}, bf16[128,4096]{1,0:T(8,128)(2,1)}) custom-call(bf16[3,128,512]{2,1,0:T(8,128)(2,1)S(1)} %get-tuple-element.55.rest_0_.refs_0_, bf16[3,128,512]{2,1,0:T(8,128)(2,1)S(1)} %collective-permute-done.15.refs_1_, ...), custom_call_target="tpu_custom_call", output_to_operand_aliasing={{0}: (2, {}), {1}: (3, {}), {2}: (4, {})} | custom-call | bytes 1024 | tf_op jit(solution)/shard_map/place/pallas_call | solution.py:275
  58.7 6.7 %collective-permute-done.14.refs_1_ = bf16[3,128,512]{2,1,0:T(8,128)(2,1)S(1)} collective-permute-done((bf16[3,128,512]{2,1,0:T(8,128)(2,1)S(1)}, bf16[3,128,512]{2,1,0:T(8,128)(2,1)S(1)}, u32[]{:S(2)}, u32[]{:S(2)}) %collective-permute-start.14) | collective-permute-done | bytes 393248 | tf_op jit(solution)/shard_map/ppermute | solution.py:224
  65.4 0.9 %place.7 = (bf16[128,4096]{1,0:T(8,128)(2,1)}, bf16[128,4096]{1,0:T(8,128)(2,1)}, bf16[128,4096]{1,0:T(8,128)(2,1)}) custom-call(bf16[3,128,512]{2,1,0:T(8,128)(2,1)S(1)} %get-tuple-element.57.refs_0_, bf16[3,128,512]{2,1,0:T(8,128)(2,1)S(1)} %collective-permute-done.14.refs_1_, ...), custom_call_target="tpu_custom_call", output_to_operand_aliasing={{0}: (2, {}), {1}: (3, {}), {2}: (4, {})} | custom-call | bytes 1024 | tf_op jit(solution)/shard_map/place/pallas_call | solution.py:275
Async XLA Ops:
  0.6 0.7 copy-start.4
  4.6 2.1 %collective-permute-start = (f32[8,128,128]{2,1,0:T(8,128)S(1)}, f32[8,128,128]{2,1,0:T(8,128)S(1)}, u32[]{:S(2)}, u32[]{:S(2)}) collective-permute-start(f32[8,128,128]{2,1,0:T(8,128)S(1)} %get-tuple-element.38), channel_id=1, source_target_pairs={{0,2},{2,0},{4,6},{6,4},{8,10},{10,8},{12,14},{14,12},{16,18},{18,... | collective-permute-start | bytes 1572872 | tf_op jit(solution)/shard_map/ppermute | solution.py:212
  5.1 13.1 %collective-permute-start.3 = (f32[8,128,128]{2,1,0:T(8,128)S(1)}, f32[8,128,128]{2,1,0:T(8,128)S(1)}, u32[]{:S(2)}, u32[]{:S(2)}) collective-permute-start(f32[8,128,128]{2,1,0:T(8,128)S(1)} %get-tuple-element.37.kept), channel_id=1, source_target_pairs={{0,2},{2,0},{4,6},{6,4},{8,10},{10,8},{12,14},{14,12},{16,18},{18,... | collective-permute-start | bytes 1572872 | tf_op jit(solution)/shard_map/ppermute | solution.py:212
  7.3 10.9 %collective-permute-start.5 = (bf16[8,128,128]{2,1,0:T(8,128)(2,1)S(1)}, bf16[8,128,128]{2,1,0:T(8,128)(2,1)S(1)}, u32[]{:S(2)}, u32[]{:S(2)}) collective-permute-start(bf16[8,128,128]{2,1,0:T(8,128)(2,1)S(1)} %pair.2.rest_0_), channel_id=1, source_target_pairs={{0,10},{4,14},{8,18},{12,22},{16,26},{20,30},{10,0},{14,4},{18,8},... | collective-permute-start | bytes 786440 | tf_op jit(solution)/shard_map/ppermute | solution.py:218
  11.9 8.6 %collective-permute-start.4 = (bf16[8,128,128]{2,1,0:T(8,128)(2,1)S(1)}, bf16[8,128,128]{2,1,0:T(8,128)(2,1)S(1)}, u32[]{:S(2)}, u32[]{:S(2)}) collective-permute-start(bf16[8,128,128]{2,1,0:T(8,128)(2,1)S(1)} %pair.2.rest_0_), channel_id=1, source_target_pairs={{0,6},{4,10},{8,14},{12,18},{16,22},{20,26},{24,30},{6,0},{10,4},{... | collective-permute-start | bytes 786440 | tf_op jit(solution)/shard_map/ppermute | solution.py:218
  13.8 9.0 %copy-start.1 = (bf16[256,2048]{1,0:T(8,128)(2,1)S(1)}, bf16[256,2048]{1,0:T(8,128)(2,1)}, u32[]{:S(2)}) copy-start(bf16[256,2048]{1,0:T(8,128)(2,1)} %k.11) | copy-start | bytes 3145732
  13.8 9.0 %copy-start.2 = (bf16[256,2048]{1,0:T(8,128)(2,1)S(1)}, bf16[256,2048]{1,0:T(8,128)(2,1)}, u32[]{:S(2)}) copy-start(bf16[256,2048]{1,0:T(8,128)(2,1)} %v.11) | copy-start | bytes 3145732
  13.8 9.0 %copy-start.3 = (bf16[256,2048]{1,0:T(8,128)(2,1)S(1)}, bf16[256,2048]{1,0:T(8,128)(2,1)}, u32[]{:S(2)}) copy-start(bf16[256,2048]{1,0:T(8,128)(2,1)} %g.11) | copy-start | bytes 3145732
  17.4 5.4 %copy-start = (bf16[256,2048]{1,0:T(8,128)(2,1)S(1)}, bf16[256,2048]{1,0:T(8,128)(2,1)}, u32[]{:S(2)}) copy-start(bf16[256,2048]{1,0:T(8,128)(2,1)} %q.11) | copy-start | bytes 3145732
  17.4 9.1 %collective-permute-start.2 = (f32[8,128,128]{2,1,0:T(8,128)S(1)}, f32[8,128,128]{2,1,0:T(8,128)S(1)}, u32[]{:S(2)}, u32[]{:S(2)}) collective-permute-start(f32[8,128,128]{2,1,0:T(8,128)S(1)} %get-tuple-element.43), channel_id=1, source_target_pairs={{0,2},{2,0},{4,6},{6,4},{8,10},{10,8},{12,14},{14,12},{16,18},{18,... | collective-permute-start | bytes 1572872 | tf_op jit(solution)/shard_map/ppermute | solution.py:212
  21.2 1.6 %collective-permute-start.6 = (f32[4,128,128]{2,1,0:T(8,128)S(1)}, f32[4,128,128]{2,1,0:T(8,128)S(1)}, u32[]{:S(2)}, u32[]{:S(2)}) collective-permute-start(f32[4,128,128]{2,1,0:T(8,128)S(1)} %get-tuple-element.45), channel_id=1, source_target_pairs={{0,2},{2,0},{4,6},{6,4},{8,10},{10,8},{12,14},{14,12},{16,18},{18,... | collective-permute-start | bytes 786440 | tf_op jit(solution)/shard_map/ppermute | solution.py:212
  21.3 16.1 %collective-permute-start.1 = (f32[8,128,128]{2,1,0:T(8,128)S(1)}, f32[8,128,128]{2,1,0:T(8,128)S(1)}, u32[]{:S(2)}, u32[]{:S(2)}) collective-permute-start(f32[8,128,128]{2,1,0:T(8,128)S(1)} %get-tuple-element.42.kept), channel_id=1, source_target_pairs={{0,2},{2,0},{4,6},{6,4},{8,10},{10,8},{12,14},{14,12},{16,18},{18,... | collective-permute-start | bytes 1572872 | tf_op jit(solution)/shard_map/ppermute | solution.py:212
  25.0 16.3 %collective-permute-start.9 = (bf16[3,128,512]{2,1,0:T(8,128)(2,1)S(1)}, bf16[3,128,512]{2,1,0:T(8,128)(2,1)S(1)}, u32[]{:S(2)}, u32[]{:S(2)}) collective-permute-start(bf16[3,128,512]{2,1,0:T(8,128)(2,1)S(1)} %get-tuple-element.47), channel_id=1, source_target_pairs={{0,1},{1,0},{2,3},{3,2},{4,5},{5,4},{6,7},{7,6},{8,9},{9,8},{10,11... | collective-permute-start | bytes 1179656 | tf_op jit(solution)/shard_map/ppermute | solution.py:224
  26.6 8.1 %collective-permute-start.12 = (f32[4,128,128]{2,1,0:T(8,128)S(1)}, f32[4,128,128]{2,1,0:T(8,128)S(1)}, u32[]{:S(2)}, u32[]{:S(2)}) collective-permute-start(f32[4,128,128]{2,1,0:T(8,128)S(1)} %get-tuple-element.53), channel_id=1, source_target_pairs={{0,2},{2,0},{4,6},{6,4},{8,10},{10,8},{12,14},{14,12},{16,18},{18,... | collective-permute-start | bytes 786440 | tf_op jit(solution)/shard_map/ppermute | solution.py:212
  27.2 10.2 %collective-permute-start.8 = (bf16[8,128,128]{2,1,0:T(8,128)(2,1)S(1)}, bf16[8,128,128]{2,1,0:T(8,128)(2,1)S(1)}, u32[]{:S(2)}, u32[]{:S(2)}) collective-permute-start(bf16[8,128,128]{2,1,0:T(8,128)(2,1)S(1)} %pair.3), channel_id=1, source_target_pairs={{0,10},{4,14},{8,18},{12,22},{16,26},{20,30},{10,0},{14,4},{18,8},... | collective-permute-start | bytes 786440 | tf_op jit(solution)/shard_map/ppermute | solution.py:218
  32.7 8.6 %collective-permute-start.7 = (bf16[8,128,128]{2,1,0:T(8,128)(2,1)S(1)}, bf16[8,128,128]{2,1,0:T(8,128)(2,1)S(1)}, u32[]{:S(2)}, u32[]{:S(2)}) collective-permute-start(bf16[8,128,128]{2,1,0:T(8,128)(2,1)S(1)} %pair.3), channel_id=1, source_target_pairs={{0,6},{4,10},{8,14},{12,18},{16,22},{20,26},{24,30},{6,0},{10,4},{... | collective-permute-start | bytes 786440 | tf_op jit(solution)/shard_map/ppermute | solution.py:218
  36.8 9.6 %collective-permute-start.13 = (bf16[3,128,512]{2,1,0:T(8,128)(2,1)S(1)}, bf16[3,128,512]{2,1,0:T(8,128)(2,1)S(1)}, u32[]{:S(2)}, u32[]{:S(2)}) collective-permute-start(bf16[3,128,512]{2,1,0:T(8,128)(2,1)S(1)} %get-tuple-element.56), channel_id=1, source_target_pairs={{0,1},{1,0},{2,3},{3,2},{4,5},{5,4},{6,7},{7,6},{8,9},{9,8},{10,11... | collective-permute-start | bytes 1179656 | tf_op jit(solution)/shard_map/ppermute | solution.py:224
  42.0 1.6 %collective-permute-start.11 = (f32[4,128,128]{2,1,0:T(8,128)S(1)}, f32[4,128,128]{2,1,0:T(8,128)S(1)}, u32[]{:S(2)}, u32[]{:S(2)}) collective-permute-start(f32[4,128,128]{2,1,0:T(8,128)S(1)} %get-tuple-element.51), channel_id=1, source_target_pairs={{0,2},{2,0},{4,6},{6,4},{8,10},{10,8},{12,14},{14,12},{16,18},{18,... | collective-permute-start | bytes 786440 | tf_op jit(solution)/shard_map/ppermute | solution.py:212
  42.1 4.3 %collective-permute-start.10 = (f32[4,128,128]{2,1,0:T(8,128)S(1)}, f32[4,128,128]{2,1,0:T(8,128)S(1)}, u32[]{:S(2)}, u32[]{:S(2)}) collective-permute-start(f32[4,128,128]{2,1,0:T(8,128)S(1)} %get-tuple-element.49), channel_id=1, source_target_pairs={{0,2},{2,0},{4,6},{6,4},{8,10},{10,8},{12,14},{14,12},{16,18},{18,... | collective-permute-start | bytes 786440 | tf_op jit(solution)/shard_map/ppermute | solution.py:212
  45.8 12.0 %collective-permute-start.15 = (bf16[3,128,512]{2,1,0:T(8,128)(2,1)S(1)}, bf16[3,128,512]{2,1,0:T(8,128)(2,1)S(1)}, u32[]{:S(2)}, u32[]{:S(2)}) collective-permute-start(bf16[3,128,512]{2,1,0:T(8,128)(2,1)S(1)} %get-tuple-element.59), channel_id=1, source_target_pairs={{0,1},{1,0},{2,3},{3,2},{4,5},{5,4},{6,7},{7,6},{8,9},{9,8},{10,11... | collective-permute-start | bytes 1179656 | tf_op jit(solution)/shard_map/ppermute | solution.py:224
  48.5 16.9 %collective-permute-start.14 = (bf16[3,128,512]{2,1,0:T(8,128)(2,1)S(1)}, bf16[3,128,512]{2,1,0:T(8,128)(2,1)S(1)}, u32[]{:S(2)}, u32[]{:S(2)}) collective-permute-start(bf16[3,128,512]{2,1,0:T(8,128)(2,1)S(1)} %get-tuple-element.58), channel_id=1, source_target_pairs={{0,1},{1,0},{2,3},{3,2},{4,5},{5,4},{6,7},{7,6},{8,9},{9,8},{10,11... | collective-permute-start | bytes 1179656 | tf_op jit(solution)/shard_map/ppermute | solution.py:224
